TPU v7x, 512 devices: a whole 4x8x8 slice. The times are simulated.
512 devices in a mesh: seq: 64 (over z, y_hi, x), head: 8 (over y_lo, core).
Axes of the slice: x: 4, y: 8 (y_hi: 2, y_lo: 4; y = y_hi * 4 + y_lo), z: 8, core: 2. Of those that a mesh axis runs over, the one named last changes fastest.
Arguments:
- query_input: bfloat16 [57344, 4096], P(('seq', 'head')), may hold values from -12 to 12
- encoded_keys: bfloat16 [57344, 1024], P(('seq', 'head')), may hold values from -8 to 8
- input_values: bfloat16 [57344, 1024], P(('seq', 'head')), may hold values from -6 to 6
- sources: int32 [64, 3], P('seq'), may hold values from -1 to 62, as said below
Outputs:
- attended: bfloat16 [57344, 4096], P(('seq', 'head'))
Inputs may be any that keep to these rules, and one draw needn't show every extreme that they name: `sources`: row c: column 0 is c - 1; columns 1 and 2 are c - 2**a and c - 2**b for two different a, b >= 1 with 2**a and 2**b below 64; an entry is -1 where that value is negative.
All inputs are finite; a program needn't handle non-finite values.
Results may differ from a plain program's by a relative error of at most 0.006.
Values may be sent and summed in bfloat16 or wider, within the bound.
No kernel may reach another device: no remote copies, remote signals or barrier semaphores. Data moves between devices by JAX's collectives and lax.ppermute only.
A program may use at most 64 MiB of HBM per device.

v0:
```python
from functools import reduce

import jax
import jax.numpy as jnp
from jax import lax
from jax.sharding import PartitionSpec as P

HEAD_SIZE = 128


negative_fill = -1e30


def passed_along(value, axis, by):
    devices = lax.axis_size(axis)
    pairs = [(i, i + by) for i in range(devices) if 0 <= i + by < devices]
    return lax.ppermute(value, axis, pairs)


def block_terms(query_head, key_head, value_head, causal):
    scores = lax.dot_general(
        query_head, key_head, (((1,), (1,)), ((), ())), preferred_element_type=jnp.float32
    ) * HEAD_SIZE ** (-0.5)
    if causal:
        position = jnp.arange(query_head.shape[0])
        allowed = position[:, None] >= position[None, :]
        scores = jnp.where(allowed, scores, negative_fill)
    highest = jnp.max(scores, axis=-1)
    weights = jnp.exp(scores - highest[:, None]).astype(jnp.bfloat16)
    row_total = jnp.sum(weights.astype(jnp.float32), axis=-1)
    partial_out = jnp.dot(weights, value_head, preferred_element_type=jnp.float32)
    return (highest, row_total, partial_out)


def combine(block_list, validity):
    maxima = [
        jnp.where(is_valid, block_term[0], negative_fill)
        for block_term, is_valid in zip(block_list, validity)
    ]
    overall = reduce(jnp.maximum, maxima)
    weighted = jnp.zeros(block_list[0][2].shape, jnp.float32)
    normalizer = jnp.zeros(block_list[0][1].shape, jnp.float32)
    for block_term, is_valid in zip(block_list, validity):
        factor = jnp.where(is_valid, jnp.exp(block_term[0] - overall), 0.0)
        weighted = weighted + factor[:, None] * block_term[2]
        normalizer = normalizer + factor * block_term[1]
    return weighted / normalizer[:, None]


def per_device(query_input, encoded_keys, input_values, sources):
    local_query, local_key, local_value = (
        lax.all_to_all(query_input, "head", split_axis=1, concat_axis=0, tiled=True),
        lax.all_to_all(encoded_keys, "head", split_axis=1, concat_axis=0, tiled=True),
        lax.all_to_all(input_values, "head", split_axis=1, concat_axis=0, tiled=True),
    )
    length = local_query.shape[0]
    query_heads = local_query.shape[1] // HEAD_SIZE
    key_value = jnp.stack([local_key, local_value])
    column_heads = key_value.shape[2] // HEAD_SIZE
    sharing = query_heads // column_heads
    span_count = lax.axis_size("seq")
    own_index = lax.axis_index("seq")
    previous = passed_along(key_value, "seq", 1)
    distances = [2**power for power in range(1, 31) if 2**power < span_count]
    fetched = [passed_along(key_value, "seq", distance) for distance in distances]
    source_row = sources[0]
    distance_table = jnp.array(distances, jnp.int32)

    def select_far(column):
        distance_away = own_index - source_row[column]
        slot_number = jnp.sum((distance_table < distance_away).astype(jnp.int32))
        chosen = fetched[0]
        for candidate_number in range(1, len(fetched)):
            chosen = jnp.where(slot_number == candidate_number, fetched[candidate_number], chosen)
        return chosen

    remotes = [
        (previous, source_row[0] >= 0),
        (select_far(1), source_row[1] >= 0),
        (select_far(2), source_row[2] >= 0),
    ]

    def one_head(head_number):
        query_head = lax.dynamic_slice_in_dim(local_query, head_number * HEAD_SIZE, HEAD_SIZE, 1)
        offset = head_number // sharing * HEAD_SIZE
        own_key = key_value[0]
        own_value = key_value[1]
        block_list = [block_terms(query_head, own_key, own_value, True)]
        validity = [jnp.array(True)]
        for remote, is_valid in remotes:
            key_head = remote[0]
            value_head = remote[1]
            block_term = block_terms(query_head, key_head, value_head, False)
            block_list.append(block_term)
            validity.append(is_valid)
        return combine(block_list, validity).astype(jnp.bfloat16)

    def write_head(head_number, output):
        return lax.dynamic_update_slice_in_dim(
            output, one_head(head_number), head_number * HEAD_SIZE, 1
        )

    attended = lax.fori_loop(
        0, query_heads, write_head, jnp.zeros((length, query_heads * HEAD_SIZE), jnp.bfloat16)
    )
    return lax.all_to_all(attended, "head", split_axis=0, concat_axis=1, tiled=True)


def solution(mesh):
    in_specs = (
        P(("seq", "head"), None),
        P(("seq", "head"), None),
        P(("seq", "head"), None),
        P("seq", None),
    )
    out_specs = P(("seq", "head"), None)
    return jax.shard_map(
        per_device, mesh=mesh, in_specs=in_specs, out_specs=out_specs, check_vma=False
    )
```

profile of v0, /device:TPU:134, one launch (start us, length us, event | category | flops | bytes accessed | tf_op | source)
XLA Modules:
  0.0 193.7 jit_solution(5505548043884570264)
XLA Ops:
  0.0 0.9 copy-done
  1.7 4.9 %all-to-all-start.1 = ((bf16[112,8,128]{2,0,1:T(8,128)(2,1)}), bf16[112,8,128]{2,0,1:T(8,128)(2,1)S(1)}, u32[]{:S(2)}, u32[]{:S(2)}) async-start(bf16[112,8,128]{2,0,1:T(8,128)(2,1)} %copy_bitcast_fusion.2), calls=%async_computation.1 | async-start | bytes 458752 | tf_op jit(solution)/shard_map/all_to_all | solution.py:53
  6.5 1.7 copy_bitcast_fusion.1
  8.2 7.4 %all-to-all-done.1 = bf16[112,8,128]{2,0,1:T(8,128)(2,1)S(1)} async-done(((bf16[112,8,128]{2,0,1:T(8,128)(2,1)}), bf16[112,8,128]{2,0,1:T(8,128)(2,1)S(1)}, u32[]{:S(2)}, u32[]{:S(2)}) %all-to-all-start.1) | async-done | bytes 229408 | tf_op jit(solution)/shard_map/all_to_all | solution.py:53
  15.6 3.4 %all-to-all-start.2 = ((bf16[112,8,128]{2,0,1:T(8,128)(2,1)}), bf16[112,8,128]{2,0,1:T(8,128)(2,1)S(1)}, u32[]{:S(2)}, u32[]{:S(2)}) async-start(bf16[112,8,128]{2,0,1:T(8,128)(2,1)} %copy_bitcast_fusion.1), calls=%async_computation.2 | async-start | bytes 458752 | tf_op jit(solution)/shard_map/all_to_all | solution.py:54
  19.0 2.2 %copy.24 = bf16[14,8,8,512]{3,2,0,1:T(8,128)(2,1)} copy(bf16[14,8,8,512]{3,2,1,0:T(8,128)(2,1)} %bitcast.83) | data formatting | bytes 1835008 | tf_op jit(solution)/shard_map/all_to_all | solution.py:52
  21.2 6.8 %all-to-all-done.2 = bf16[112,8,128]{2,0,1:T(8,128)(2,1)S(1)} async-done(((bf16[112,8,128]{2,0,1:T(8,128)(2,1)}), bf16[112,8,128]{2,0,1:T(8,128)(2,1)S(1)}, u32[]{:S(2)}, u32[]{:S(2)}) %all-to-all-start.2) | async-done | bytes 229408 | tf_op jit(solution)/shard_map/all_to_all | solution.py:54
  28.0 3.6 %all-to-all-start = ((bf16[112,8,512]{2,0,1:T(8,128)(2,1)}), bf16[112,8,512]{2,0,1:T(8,128)(2,1)S(1)}, u32[]{:S(2)}, u32[]{:S(2)}) async-start(bf16[112,8,512]{2,0,1:T(8,128)(2,1)} %bitcast.59), calls=%async_computation | async-start | bytes 1835008 | tf_op jit(solution)/shard_map/all_to_all | solution.py:52
  32.3 7.0 %collective-permute-start.5 = (bf16[2,896,128]{2,1,0:T(8,128)(2,1)}, bf16[2,896,128]{2,1,0:T(8,128)(2,1)S(1)}, u32[]{:S(2)}, u32[]{:S(2)}) collective-permute-start(bf16[2,896,128]{2,1,0:T(8,128)(2,1)} %pad_maximum_fusion), channel_id=1, source_target_pairs={{0,16},{8,24},{16,32},{24,40},{32,48},{40,56},{48,64},{56,72},{64,... | collective-permute-start | bytes 1376264 | tf_op jit(solution)/shard_map/ppermute | solution.py:17
  39.3 5.4 %collective-permute-start.4 = (bf16[2,896,128]{2,1,0:T(8,128)(2,1)}, bf16[2,896,128]{2,1,0:T(8,128)(2,1)S(1)}, u32[]{:S(2)}, u32[]{:S(2)}) collective-permute-start(bf16[2,896,128]{2,1,0:T(8,128)(2,1)} %pad_maximum_fusion), channel_id=1, source_target_pairs={{0,32},{8,40},{16,48},{24,56},{32,64},{40,72},{48,80},{56,88},{64,... | collective-permute-start | bytes 1376264 | tf_op jit(solution)/shard_map/ppermute | solution.py:17
  44.7 5.5 %collective-permute-start.3 = (bf16[2,896,128]{2,1,0:T(8,128)(2,1)}, bf16[2,896,128]{2,1,0:T(8,128)(2,1)S(1)}, u32[]{:S(2)}, u32[]{:S(2)}) collective-permute-start(bf16[2,896,128]{2,1,0:T(8,128)(2,1)} %pad_maximum_fusion), channel_id=1, source_target_pairs={{0,64},{8,72},{16,80},{24,88},{32,96},{40,104},{48,112},{56,120},{... | collective-permute-start | bytes 1376264 | tf_op jit(solution)/shard_map/ppermute | solution.py:17
  50.2 4.3 %collective-permute-start.2 = (bf16[2,896,128]{2,1,0:T(8,128)(2,1)}, bf16[2,896,128]{2,1,0:T(8,128)(2,1)}, u32[]{:S(2)}, u32[]{:S(2)}) collective-permute-start(bf16[2,896,128]{2,1,0:T(8,128)(2,1)} %pad_maximum_fusion), channel_id=1, source_target_pairs={{0,128},{8,136},{16,144},{24,152},{32,160},{40,168},{48,176},{56,1... | collective-permute-start | bytes 1376264 | tf_op jit(solution)/shard_map/ppermute | solution.py:17
  54.5 2.4 %collective-permute-start.1 = (bf16[2,896,128]{2,1,0:T(8,128)(2,1)}, bf16[2,896,128]{2,1,0:T(8,128)(2,1)}, u32[]{:S(2)}, u32[]{:S(2)}) collective-permute-start(bf16[2,896,128]{2,1,0:T(8,128)(2,1)} %pad_maximum_fusion), channel_id=1, source_target_pairs={{0,256},{8,264},{16,272},{24,280},{32,288},{40,296},{48,304},{56,3... | collective-permute-start | bytes 1376264 | tf_op jit(solution)/shard_map/ppermute | solution.py:17
  57.0 30.2 %collective-permute-done.5 = bf16[2,896,128]{2,1,0:T(8,128)(2,1)S(1)} collective-permute-done((bf16[2,896,128]{2,1,0:T(8,128)(2,1)}, bf16[2,896,128]{2,1,0:T(8,128)(2,1)S(1)}, u32[]{:S(2)}, u32[]{:S(2)}) %collective-permute-start.5) | collective-permute-done | bytes 458784 | tf_op jit(solution)/shard_map/ppermute | solution.py:17
  87.1 1.9 collective-permute-start
  98.5 2.8 %collective-permute-done.4 = bf16[2,896,128]{2,1,0:T(8,128)(2,1)S(1)} collective-permute-done((bf16[2,896,128]{2,1,0:T(8,128)(2,1)}, bf16[2,896,128]{2,1,0:T(8,128)(2,1)S(1)}, u32[]{:S(2)}, u32[]{:S(2)}) %collective-permute-start.4) | collective-permute-done | bytes 458784 | tf_op jit(solution)/shard_map/ppermute | solution.py:17
  101.4 20.4 %collective-permute-done.2 = bf16[2,896,128]{2,1,0:T(8,128)(2,1)} collective-permute-done((bf16[2,896,128]{2,1,0:T(8,128)(2,1)}, bf16[2,896,128]{2,1,0:T(8,128)(2,1)}, u32[]{:S(2)}, u32[]{:S(2)}) %collective-permute-start.2) | collective-permute-done | bytes 458784 | tf_op jit(solution)/shard_map/ppermute | solution.py:17
  121.8 8.7 %collective-permute-done.1 = bf16[2,896,128]{2,1,0:T(8,128)(2,1)} collective-permute-done((bf16[2,896,128]{2,1,0:T(8,128)(2,1)}, bf16[2,896,128]{2,1,0:T(8,128)(2,1)}, u32[]{:S(2)}, u32[]{:S(2)}) %collective-permute-start.1) | collective-permute-done | bytes 458784 | tf_op jit(solution)/shard_map/ppermute | solution.py:17
  130.5 1.6 select_select_fusion
  132.2 33.4 %while.13 = (s32[]{:T(128)}, bf16[896,512]{1,0:T(8,128)(2,1)S(1)}, bf16[896,512]{1,0:T(8,128)(2,1)S(1)}, bf16[896,128]{1,0:T(8,128)(2,1)}, pred[]{:T(512)}, /*in...) while((s32[]{:T(128)}, bf16[896,512]{1,0:T(8,128)(2,1)S(1)}, ...), condition=%wide.region_11.12_spmd, body=%wide.region_2.11_spmd.sunk | while | flops 1682139648 | bytes 45312748 | solution.py:103
  132.2 1.5 fusion.55
  135.0 1.1 convert_reduce_fusion.6
  136.6 0.9 convert_reduce_fusion.7
  140.6 1.5 fusion.55
  143.3 1.1 convert_reduce_fusion.6
  145.0 0.9 convert_reduce_fusion.7
  148.9 1.5 fusion.55
  151.6 1.1 convert_reduce_fusion.6
  157.2 1.5 fusion.55
  160.0 1.1 convert_reduce_fusion.6
  165.6 27.1 %all_to_all.76 = bf16[8,112,512]{2,1,0:T(8,128)(2,1)S(1)} all-to-all(bf16[8,112,512]{2,1,0:T(8,128)(2,1)S(1)} %bitcast.77), channel_id=1, replica_groups=mesh['seq'=64,'head'=8] {'head'}, dimensions={0} | all-to-all | bytes 1835008 | tf_op jit(solution)/shard_map/all_to_all | solution.py:106
  192.6 1.0 copy.20
  (63 shorter events, 23.7 us)
Async XLA Ops:
  0.0 0.9 copy-start
  0.0 92.1 %copy-start.7 = (s32[5]{0:T(128)S(1)}, s32[5]{0:T(128)}, u32[]{:S(2)}) copy-start(s32[5]{0:T(128)} %constant.77.clone) | copy-start | bytes 64
  0.9 88.1 %copy-start.6 = (s32[1,3]{1,0:T(1,128)S(1)}, s32[1,3]{1,0:T(1,128)}, u32[]{:S(2)}) copy-start(s32[1,3]{1,0:T(1,128)} %param.10) | copy-start | bytes 40
  1.7 13.9 %all-to-all-start.1 = ((bf16[112,8,128]{2,0,1:T(8,128)(2,1)}), bf16[112,8,128]{2,0,1:T(8,128)(2,1)S(1)}, u32[]{:S(2)}, u32[]{:S(2)}) async-start(bf16[112,8,128]{2,0,1:T(8,128)(2,1)} %copy_bitcast_fusion.2), calls=%async_computation.1 | async-start | bytes 458752 | tf_op jit(solution)/shard_map/all_to_all | solution.py:53
  15.6 116.5 %copy-start.1 = (bf16[112,8,128]{2,0,1:T(8,128)(2,1)}, bf16[112,8,128]{2,0,1:T(8,128)(2,1)S(1)}, u32[]{:S(2)}) copy-start(bf16[112,8,128]{2,0,1:T(8,128)(2,1)S(1)} %all-to-all-done.1) | copy-start | bytes 688132
  15.6 12.4 %all-to-all-start.2 = ((bf16[112,8,128]{2,0,1:T(8,128)(2,1)}), bf16[112,8,128]{2,0,1:T(8,128)(2,1)S(1)}, u32[]{:S(2)}, u32[]{:S(2)}) async-start(bf16[112,8,128]{2,0,1:T(8,128)(2,1)} %copy_bitcast_fusion.1), calls=%async_computation.2 | async-start | bytes 458752 | tf_op jit(solution)/shard_map/all_to_all | solution.py:54
  28.0 104.2 %copy-start.2 = (bf16[112,8,128]{2,0,1:T(8,128)(2,1)}, bf16[112,8,128]{2,0,1:T(8,128)(2,1)S(1)}, u32[]{:S(2)}) copy-start(bf16[112,8,128]{2,0,1:T(8,128)(2,1)S(1)} %all-to-all-done.2) | copy-start | bytes 688132
  28.0 104.2 %all-to-all-start = ((bf16[112,8,512]{2,0,1:T(8,128)(2,1)}), bf16[112,8,512]{2,0,1:T(8,128)(2,1)S(1)}, u32[]{:S(2)}, u32[]{:S(2)}) async-start(bf16[112,8,512]{2,0,1:T(8,128)(2,1)} %bitcast.59), calls=%async_computation | async-start | bytes 1835008 | tf_op jit(solution)/shard_map/all_to_all | solution.py:52
  32.3 54.8 %collective-permute-start.5 = (bf16[2,896,128]{2,1,0:T(8,128)(2,1)}, bf16[2,896,128]{2,1,0:T(8,128)(2,1)S(1)}, u32[]{:S(2)}, u32[]{:S(2)}) collective-permute-start(bf16[2,896,128]{2,1,0:T(8,128)(2,1)} %pad_maximum_fusion), channel_id=1, source_target_pairs={{0,16},{8,24},{16,32},{24,40},{32,48},{40,56},{48,64},{56,72},{64,... | collective-permute-start | bytes 1376264 | tf_op jit(solution)/shard_map/ppermute | solution.py:17
  39.3 62.0 %collective-permute-start.4 = (bf16[2,896,128]{2,1,0:T(8,128)(2,1)}, bf16[2,896,128]{2,1,0:T(8,128)(2,1)S(1)}, u32[]{:S(2)}, u32[]{:S(2)}) collective-permute-start(bf16[2,896,128]{2,1,0:T(8,128)(2,1)} %pad_maximum_fusion), channel_id=1, source_target_pairs={{0,32},{8,40},{16,48},{24,56},{32,64},{40,72},{48,80},{56,88},{64,... | collective-permute-start | bytes 1376264 | tf_op jit(solution)/shard_map/ppermute | solution.py:17
  44.7 56.6 %collective-permute-start.3 = (bf16[2,896,128]{2,1,0:T(8,128)(2,1)}, bf16[2,896,128]{2,1,0:T(8,128)(2,1)S(1)}, u32[]{:S(2)}, u32[]{:S(2)}) collective-permute-start(bf16[2,896,128]{2,1,0:T(8,128)(2,1)} %pad_maximum_fusion), channel_id=1, source_target_pairs={{0,64},{8,72},{16,80},{24,88},{32,96},{40,104},{48,112},{56,120},{... | collective-permute-start | bytes 1376264 | tf_op jit(solution)/shard_map/ppermute | solution.py:17
  50.2 71.6 %collective-permute-start.2 = (bf16[2,896,128]{2,1,0:T(8,128)(2,1)}, bf16[2,896,128]{2,1,0:T(8,128)(2,1)}, u32[]{:S(2)}, u32[]{:S(2)}) collective-permute-start(bf16[2,896,128]{2,1,0:T(8,128)(2,1)} %pad_maximum_fusion), channel_id=1, source_target_pairs={{0,128},{8,136},{16,144},{24,152},{32,160},{40,168},{48,176},{56,1... | collective-permute-start | bytes 1376264 | tf_op jit(solution)/shard_map/ppermute | solution.py:17
  54.5 76.0 %collective-permute-start.1 = (bf16[2,896,128]{2,1,0:T(8,128)(2,1)}, bf16[2,896,128]{2,1,0:T(8,128)(2,1)}, u32[]{:S(2)}, u32[]{:S(2)}) collective-permute-start(bf16[2,896,128]{2,1,0:T(8,128)(2,1)} %pad_maximum_fusion), channel_id=1, source_target_pairs={{0,256},{8,264},{16,272},{24,280},{32,288},{40,296},{48,304},{56,3... | collective-permute-start | bytes 1376264 | tf_op jit(solution)/shard_map/ppermute | solution.py:17
  87.1 45.0 %collective-permute-start = (bf16[2,896,128]{2,1,0:T(8,128)(2,1)}, bf16[2,896,128]{2,1,0:T(8,128)(2,1)S(1)}, u32[]{:S(2)}, u32[]{:S(2)}) collective-permute-start(bf16[2,896,128]{2,1,0:T(8,128)(2,1)} %pad_maximum_fusion), channel_id=1, source_target_pairs={{0,8},{8,16},{16,24},{24,32},{32,40},{40,48},{48,56},{56,64},{64,7... | collective-permute-start | bytes 1376264 | tf_op jit(solution)/shard_map/ppermute | solution.py:17
  101.4 20.4 %copy-start.4 = (bf16[2,896,128]{2,1,0:T(8,128)(2,1)}, bf16[2,896,128]{2,1,0:T(8,128)(2,1)S(1)}, u32[]{:S(2)}) copy-start(bf16[2,896,128]{2,1,0:T(8,128)(2,1)S(1)} %collective-permute-done.4) | copy-start | bytes 1376260
  101.4 20.4 %copy-start.5 = (bf16[2,896,128]{2,1,0:T(8,128)(2,1)}, bf16[2,896,128]{2,1,0:T(8,128)(2,1)S(1)}, u32[]{:S(2)}) copy-start(bf16[2,896,128]{2,1,0:T(8,128)(2,1)S(1)} %collective-permute-done.3) | copy-start | bytes 1376260
  136.6 1.0 copy-start.3
  145.0 1.0 copy-start.3
  153.3 1.0 copy-start.3
  161.6 1.0 copy-start.3
where the time goes:
time: 195 us; the launch traced here: 194 us
  waiting for transfers between devices  76.3 us (39%)
  starting transfers between devices  38.3 us (20%)
  blocking collectives  27.1 us (14%)
  matrix products  24.9 us (13%)
  other arithmetic  11.1 us (6%)
  between operations  8.31 us (4%)
  local copies, waits for them, and re-layouts  7.25 us (4%)
    ppermute x6, waiting for transfers between devices, passed_along(): return lax.ppermute(value, axis, pairs)  62.1 us
    all_to_all x1, blocking collectives, per_device(): lax.all_to_all(attended, 'head', split_axis=0, concat_axis=1, tiled=True)  27.1 us
    ppermute x6, starting transfers between devices, passed_along(): return lax.ppermute(value, axis, pairs)  26.5 us
    dot_general x16, matrix products, block_terms(): lax.dot_general(query_head, key_head, (((1,), (1,)), ((), ())), preferred...  13.3 us
    dot_general x16, matrix products, block_terms(): jnp.dot(weights, value_head, preferred_element_type=jnp.float32)  11.7 us
    reduce_sum x8, other arithmetic, block_terms(): row_total = jnp.sum(weights.astype(jnp.float32), axis=-1)  7.96 us
    all_to_all x1, waiting for transfers between devices, per_device(): lax.all_to_all(encoded_keys, 'head', split_axis=1, concat_axis=0, tiled=T...  7.38 us
    all_to_all x1, waiting for transfers between devices, per_device(): lax.all_to_all(input_values, 'head', split_axis=1, concat_axis=0, tiled=T...  6.77 us
  transfers between devices with their start and end apart: 9, of which 6 were waited for; matrix products, arithmetic and copies ran while one was open for 4% of the time, Pallas kernels for 0%

commit v1 on v0

v1 whole, which is shorter than its diff:
```python
import functools

import jax
import jax.numpy as jnp
import numpy as np
from jax import lax
from jax.experimental import pallas as pl
from jax.experimental.pallas import tpu as pltpu
from jax.sharding import PartitionSpec as P

HEAD_SIZE = 128
AXES = ("seq", "head")
SPANS, SLOTS, HALF, COLUMN = 64, 8, 4, 4
LOG_SCALE = float(HEAD_SIZE**-0.5 * np.log2(np.e))
EMPTY = -1e30
F32, BF16 = jnp.float32, jnp.bfloat16


def slot_order(span):
    if (span // COLUMN) % 2 == 0:
        return list(range(SLOTS))
    return [(SLOTS // 2 - 1 - slot // 2) * 2 + slot % 2 for slot in range(SLOTS)]


def exchange(value):
    groups = [[span * SLOTS + slot for slot in slot_order(span)] for span in range(SPANS)]
    return lax.all_to_all(
        value, AXES, split_axis=0, concat_axis=0, tiled=True, axis_index_groups=groups
    )


def moved(value, target):
    pairs = []
    for span in range(SPANS):
        goal = target(span)
        if goal is not None:
            here, there = slot_order(span), slot_order(goal)
            pairs += [(span * SLOTS + a, goal * SLOTS + b) for a, b in zip(here, there)]
    return lax.ppermute(value, AXES, pairs)


def ahead(distance):
    return lambda span: span + distance if span + distance < SPANS else None


def along_row(distance):
    return lambda span: span // COLUMN * COLUMN + (span + distance) % COLUMN


def scores_of(query, key):
    return lax.dot_general(query, key, (((1,), (1,)), ((), ())), preferred_element_type=F32)


def block_step(q_ref, key_ref, value_ref, top_ref, total_ref, part_ref, rows_each):
    heads = q_ref.shape[1] // HEAD_SIZE

    def rows_step(tile, _):
        rows = pl.ds(pl.multiple_of(tile * rows_each, rows_each), rows_each)

        def score(head):
            return scores_of(q_ref[rows, pl.ds(head * HEAD_SIZE, HEAD_SIZE)], key_ref[...])

        following = score(0)
        for head in range(heads):
            scores = following
            if head + 1 < heads:
                following = score(head + 1)
            lanes = pl.ds(head * HEAD_SIZE, HEAD_SIZE)
            old_top = top_ref[rows, lanes]
            top = jnp.maximum(old_top, jnp.max(scores, axis=1, keepdims=True) * LOG_SCALE)
            weights = jnp.exp2(scores * LOG_SCALE - top[:, :1]).astype(BF16)
            sums = jnp.dot(weights, value_ref[...], preferred_element_type=F32)
            factor = jnp.exp2(old_top - top)
            top_ref[rows, lanes] = top
            part_ref[rows, lanes] = part_ref[rows, lanes] * factor + sums[:, :HEAD_SIZE]
            total_ref[rows, lanes] = total_ref[rows, lanes] * factor + sums[:, HEAD_SIZE:]
        return 0

    lax.fori_loop(0, q_ref.shape[0] // rows_each, rows_step, 0)


def own_kernel(place_ref, q_ref, key_ref, value_ref, top_ref, total_ref, part_ref, wide_ref):
    mirrored = place_ref[0]
    tokens = q_ref.shape[0]
    heads = q_ref.shape[1] // HEAD_SIZE
    chunk = tokens // HALF
    wide_ref[:, :HEAD_SIZE] = value_ref[...]
    wide_ref[:, HEAD_SIZE:] = jnp.ones((tokens, HEAD_SIZE), BF16)
    order = lax.broadcasted_iota(jnp.int32, (chunk, chunk), 0)
    allowed = order >= lax.broadcasted_iota(jnp.int32, (chunk, chunk), 1)
    for turn in range(HALF):
        start = jnp.where(mirrored == 1, (HALF - 1 - turn) * chunk, turn * chunk)
        rows = pl.ds(pl.multiple_of(start, chunk), chunk)
        if turn:
            earlier = jnp.where(mirrored == 1, (HALF - turn) * chunk, 0)
            before = pl.ds(pl.multiple_of(earlier, chunk), turn * chunk)
        for head in range(heads):
            lanes = pl.ds(head * HEAD_SIZE, HEAD_SIZE)
            query = q_ref[rows, lanes]
            near = jnp.where(allowed, scores_of(query, key_ref[rows, :]), EMPTY)
            top = jnp.max(near, axis=1, keepdims=True)
            if turn:
                far = scores_of(query, key_ref[before, :])
                top = jnp.maximum(top, jnp.max(far, axis=1, keepdims=True))
            top = top * LOG_SCALE
            weights = jnp.exp2(near * LOG_SCALE - top).astype(BF16)
            sums = jnp.dot(weights, wide_ref[rows, :], preferred_element_type=F32)
            if turn:
                weights = jnp.exp2(far * LOG_SCALE - top).astype(BF16)
                sums += jnp.dot(weights, wide_ref[before, :], preferred_element_type=F32)
            top_ref[rows, lanes] = jnp.broadcast_to(top, (chunk, HEAD_SIZE))
            part_ref[rows, lanes] = sums[:, :HEAD_SIZE]
            total_ref[rows, lanes] = sums[:, HEAD_SIZE:]


def earlier_kernel(use_ref, q_ref, *refs, blocks, last):
    pairs, refs = refs[: 2 * blocks], refs[2 * blocks :]
    old, refs = refs[:3], refs[3:]
    if last:
        out_ref, top_ref, total_ref, part_ref, wide_ref, key_buffer = refs
    else:
        top_ref, total_ref, part_ref, wide_ref, key_buffer = refs
    tokens = q_ref.shape[0]
    for new_ref, old_ref in zip((top_ref, total_ref, part_ref), old):
        new_ref[...] = old_ref[...]
    wide_ref[:, HEAD_SIZE:] = jnp.ones((tokens, HEAD_SIZE), BF16)

    def one(block, _):
        @pl.when(use_ref[block] == 1)
        def _():
            for number in range(blocks):

                @pl.when(block == number)
                def _():
                    key_buffer[...] = pairs[2 * number][...]
                    wide_ref[:, :HEAD_SIZE] = pairs[2 * number + 1][...]

            block_step(q_ref, key_buffer, wide_ref, top_ref, total_ref, part_ref, tokens // HALF)

        return 0

    lax.fori_loop(0, blocks, one, 0)
    if last:
        out_ref[...] = (part_ref[...] / total_ref[...]).astype(BF16)


VMEM = pl.BlockSpec(memory_space=pltpu.VMEM)
SMEM = pl.BlockSpec(memory_space=pltpu.SMEM)
PARAMS = dict(vmem_limit_bytes=40 * 2**20)


def own_call(place, query, key, value):
    running = jax.ShapeDtypeStruct(query.shape, F32)
    wide = pltpu.VMEM((key.shape[0], 2 * HEAD_SIZE), BF16)
    return pl.pallas_call(
        own_kernel,
        out_shape=[running] * 3,
        in_specs=[SMEM, VMEM, VMEM, VMEM],
        out_specs=[VMEM] * 3,
        scratch_shapes=[wide],
        compiler_params=pltpu.CompilerParams(**PARAMS),
    )(place, query, key, value)


def earlier_call(use, query, blocks, state, last):
    running = [jax.ShapeDtypeStruct(query.shape, F32)] * 3
    scratch = [
        pltpu.VMEM((query.shape[0], 2 * HEAD_SIZE), BF16),
        pltpu.VMEM((query.shape[0], HEAD_SIZE), BF16),
    ]
    if last:
        scratch = [pltpu.VMEM(query.shape, F32)] * 3 + scratch
    arrays = [part for block in blocks for part in block]
    return pl.pallas_call(
        functools.partial(earlier_kernel, blocks=len(blocks), last=last),
        out_shape=jax.ShapeDtypeStruct(query.shape, BF16) if last else running,
        in_specs=[SMEM] + [VMEM] * (1 + len(arrays) + 3),
        out_specs=VMEM if last else [VMEM] * 3,
        scratch_shapes=scratch,
        compiler_params=pltpu.CompilerParams(**PARAMS),
    )(use, query, *arrays, *state)


def per_device(query_input, encoded_keys, input_values, sources):
    tokens = query_input.shape[0]
    span = lax.axis_index("seq")
    column = span % COLUMN
    mirrored = (span // COLUMN) % 2

    def gathered(value):
        cut = value.reshape(tokens, SLOTS, -1).transpose(1, 0, 2)
        return exchange(cut).reshape(tokens * SLOTS, -1)

    key = gathered(encoded_keys)
    value = gathered(input_values)
    query = gathered(query_input)

    def fetched(part):
        half = moved(part, ahead(4))
        eight = moved(part, ahead(8))
        far = moved(part, ahead(32))
        one = moved(jnp.where(column >= 3, half, part), along_row(1))
        two = moved(jnp.where(column >= 2, half, part), along_row(2))
        sixteen = moved(eight, ahead(8))
        return {1: one, 2: two, 4: half, 8: eight, 16: sixteen, 32: far}

    keys, values = fetched(key), fetched(value)
    row = sources[0]

    def wanted(distance):
        if distance == 1:
            return row[0] >= 0
        return jnp.any((row[1:] >= 0) & (span - row[1:] == distance))

    def use(distances):
        return jnp.stack([wanted(d) for d in distances]).astype(jnp.int32)

    state = own_call(mirrored.reshape(1).astype(jnp.int32), query, key, value)
    early, late = (8, 4, 16), (1, 2, 32)
    state = earlier_call(use(early), query, [(keys[d], values[d]) for d in early], state, False)
    attended = earlier_call(use(late), query, [(keys[d], values[d]) for d in late], state, True)
    back = exchange(attended.reshape(SLOTS, tokens, -1))
    return back.transpose(1, 0, 2).reshape(tokens, -1)


def solution(mesh):
    in_specs = (P(AXES, None), P(AXES, None), P(AXES, None), P("seq", None))
    return jax.shard_map(
        per_device, mesh=mesh, in_specs=in_specs, out_specs=P(AXES, None), check_vma=False
    )
```

time: 195 us -> 167 us (0.86)
  the two profiles are of different devices: /device:TPU:134 before, /device:TPU:132 now
where the time goes in v1:
time: 167 us; the launch traced here: 166 us
  starting transfers between devices  77.1 us (46%)
  blocking collectives  30.7 us (18%)
  Pallas kernels  26.4 us (16%)
  waiting for transfers between devices  17 us (10%)
  local copies, waits for them, and re-layouts  8.61 us (5%)
  other arithmetic  5.59 us (3%)
    ppermute x12, starting transfers between devices, moved(): return lax.ppermute(value, AXES, pairs)  65.1 us
    all_to_all x1, blocking collectives, exchange(): lax.all_to_all(value, AXES, split_axis=0, concat_axis=0, tiled=True, axis...  30.7 us
    pallas_call x2, Pallas kernels, earlier_call(): pl.pallas_call(functools.partial(earlier_kernel, blocks=len(blocks), last...  22.7 us
    all_to_all x3, waiting for transfers between devices, exchange(): lax.all_to_all(value, AXES, split_axis=0, concat_axis=0, tiled=True, axis...  15.3 us
    all_to_all x3, starting transfers between devices, exchange(): lax.all_to_all(value, AXES, split_axis=0, concat_axis=0, tiled=True, axis...  12 us
    unnamed x14, local copies, waits for them, and re-layouts  4.19 us
    pallas_call x1, Pallas kernels, own_call(): pl.pallas_call(own_kernel, out_shape=[running] * 3, in_specs=[SMEM, VMEM,...  3.72 us
  transfers between devices with their start and end apart: 15, of which 3 were waited for; matrix products, arithmetic and copies ran while one was open for 5% of the time, Pallas kernels for 7%

profile of v1, /device:TPU:132, one launch (start us, length us, event | category | flops | bytes accessed | tf_op | source)
XLA Modules:
  0.0 165.7 jit_solution(11335556726034133801)
XLA Ops:
  0.0 0.9 copy-done
  1.7 4.9 %all-to-all-start.1 = ((bf16[8,112,128]{2,1,0:T(8,128)(2,1)}), bf16[8,112,128]{2,1,0:T(8,128)(2,1)S(1)}, u32[]{:S(2)}, u32[]{:S(2)}) async-start(bf16[8,112,128]{2,1,0:T(8,128)(2,1)} %bitcast_bitcast_fusion.2), calls=%async_computation.1 | async-start | bytes 458752 | tf_op jit(solution)/shard_map/all_to_all | solution.py:27
  6.5 1.7 %bitcast_bitcast_fusion.1 = bf16[8,112,128]{2,1,0:T(8,128)(2,1)} fusion(bf16[112,1024]{1,0:T(8,128)(2,1)} %param.6), kind=kLoop, calls=%fused_computation.1 | loop fusion | bytes 458752 | tf_op jit(solution)/shard_map/transpose | solution.py:191
  8.2 7.4 %all-to-all-done.1 = bf16[8,112,128]{2,1,0:T(8,128)(2,1)S(1)} async-done(((bf16[8,112,128]{2,1,0:T(8,128)(2,1)}), bf16[8,112,128]{2,1,0:T(8,128)(2,1)S(1)}, u32[]{:S(2)}, u32[]{:S(2)}) %all-to-all-start.1) | async-done | bytes 229408 | tf_op jit(solution)/shard_map/all_to_all | solution.py:27
  15.6 3.4 %all-to-all-start.2 = ((bf16[8,112,128]{2,1,0:T(8,128)(2,1)}), bf16[8,112,128]{2,1,0:T(8,128)(2,1)S(1)}, u32[]{:S(2)}, u32[]{:S(2)}) async-start(bf16[8,112,128]{2,1,0:T(8,128)(2,1)} %bitcast_bitcast_fusion.1), calls=%async_computation.2 | async-start | bytes 458752 | tf_op jit(solution)/shard_map/all_to_all | solution.py:27
  19.0 1.0 copy.16
  20.0 7.9 %all-to-all-done.2 = bf16[8,112,128]{2,1,0:T(8,128)(2,1)S(1)} async-done(((bf16[8,112,128]{2,1,0:T(8,128)(2,1)}), bf16[8,112,128]{2,1,0:T(8,128)(2,1)S(1)}, u32[]{:S(2)}, u32[]{:S(2)}) %all-to-all-start.2) | async-done | bytes 229408 | tf_op jit(solution)/shard_map/all_to_all | solution.py:27
  28.0 3.7 %all-to-all-start = ((bf16[8,112,512]{2,1,0:T(8,128)(2,1)}), bf16[8,112,512]{2,1,0:T(8,128)(2,1)S(1)}, u32[]{:S(2)}, u32[]{:S(2)}) async-start(bf16[8,112,512]{2,1,0:T(8,128)(2,1)} %bitcast.38), calls=%async_computation | async-start | bytes 1835008 | tf_op jit(solution)/shard_map/all_to_all | solution.py:27
  31.7 4.7 %collective-permute-start = (bf16[896,128]{1,0:T(8,128)(2,1)S(1)}, bf16[896,128]{1,0:T(8,128)(2,1)S(1)}, u32[]{:S(2)}, u32[]{:S(2)}) collective-permute-start(bf16[896,128]{1,0:T(8,128)(2,1)S(1)} %bitcast.48), channel_id=1, source_target_pairs={{0,38},{1,39},{2,36},{3,37},{4,34},{5,35},{6,32},{7,33},{8,46},{9,... | collective-permute-start | bytes 688136 | tf_op jit(solution)/shard_map/ppermute | solution.py:39
  36.4 4.3 %collective-permute-start.8 = (bf16[896,128]{1,0:T(8,128)(2,1)S(1)}, bf16[896,128]{1,0:T(8,128)(2,1)S(1)}, u32[]{:S(2)}, u32[]{:S(2)}) collective-permute-start(bf16[896,128]{1,0:T(8,128)(2,1)S(1)} %bitcast.49), channel_id=1, source_target_pairs={{0,64},{1,65},{2,66},{3,67},{4,68},{5,69},{6,70},{7,71},{8,72},{9,... | collective-permute-start | bytes 688136 | tf_op jit(solution)/shard_map/ppermute | solution.py:39
  40.7 5.5 %collective-permute-start.9 = (bf16[896,128]{1,0:T(8,128)(2,1)S(1)}, bf16[896,128]{1,0:T(8,128)(2,1)S(1)}, u32[]{:S(2)}, u32[]{:S(2)}) collective-permute-start(bf16[896,128]{1,0:T(8,128)(2,1)S(1)} %bitcast.44), channel_id=1, source_target_pairs={{0,64},{1,65},{2,66},{3,67},{4,68},{5,69},{6,70},{7,71},{8,72},{9,... | collective-permute-start | bytes 688136 | tf_op jit(solution)/shard_map/ppermute | solution.py:39
  46.2 3.3 %collective-permute-start.2 = (bf16[896,128]{1,0:T(8,128)(2,1)S(1)}, bf16[896,128]{1,0:T(8,128)(2,1)S(1)}, u32[]{:S(2)}, u32[]{:S(2)}) collective-permute-start(bf16[896,128]{1,0:T(8,128)(2,1)S(1)} %bitcast.45), channel_id=1, source_target_pairs={{0,38},{1,39},{2,36},{3,37},{4,34},{5,35},{6,32},{7,33},{8,46},{9,... | collective-permute-start | bytes 688136 | tf_op jit(solution)/shard_map/ppermute | solution.py:39
  49.5 3.3 %collective-permute-start.6 = (bf16[896,128]{1,0:T(8,128)(2,1)S(1)}, bf16[896,128]{1,0:T(8,128)(2,1)S(1)}, u32[]{:S(2)}, u32[]{:S(2)}) collective-permute-start(bf16[896,128]{1,0:T(8,128)(2,1)S(1)} %bitcast.50), channel_id=1, source_target_pairs={{0,256},{1,257},{2,258},{3,259},{4,260},{5,261},{6,262},{7,263},{8... | collective-permute-start | bytes 688136 | tf_op jit(solution)/shard_map/ppermute | solution.py:39
  52.8 1.3 collective-permute-start.7
  54.1 0.8 broadcast_select_fusion.1
  54.9 3.1 %collective-permute-start.1 = (bf16[896,128]{1,0:T(8,128)(2,1)}, bf16[896,128]{1,0:T(8,128)(2,1)S(1)}, u32[]{:S(2)}, u32[]{:S(2)}) collective-permute-start(bf16[896,128]{1,0:T(8,128)(2,1)} %get-tuple-element.25), channel_id=1, source_target_pairs={{0,8},{1,9},{2,10},{3,11},{4,12},{5,13},{6,14},{7,15},{8,16},{9,17... | collective-permute-start | bytes 688136 | tf_op jit(solution)/shard_map/ppermute | solution.py:39
  58.0 1.7 %collective-permute-done.9.refs_1_ = bf16[896,128]{1,0:T(8,128)(2,1)S(1)} collective-permute-done((bf16[896,128]{1,0:T(8,128)(2,1)S(1)}, bf16[896,128]{1,0:T(8,128)(2,1)S(1)}, u32[]{:S(2)}, u32[]{:S(2)}) %collective-permute-start.9) | collective-permute-done | bytes 229408 | tf_op jit(solution)/shard_map/ppermute | solution.py:39
  59.7 23.6 %collective-permute-start.10 = (bf16[896,128]{1,0:T(8,128)(2,1)S(1)}, bf16[896,128]{1,0:T(8,128)(2,1)S(1)}, u32[]{:S(2)}, u32[]{:S(2)}) collective-permute-start(bf16[896,128]{1,0:T(8,128)(2,1)S(1)} %collective-permute-done.8.refs_0_), channel_id=1, source_target_pairs={{0,64},{1,65},{2,66},{3,67},{4,68},{5,69},{6,70},{7,71},{8,72},{9,... | collective-permute-start | bytes 688136 | tf_op jit(solution)/shard_map/ppermute | solution.py:39
  83.4 5.6 %collective-permute-start.11 = (bf16[896,128]{1,0:T(8,128)(2,1)S(1)}, bf16[896,128]{1,0:T(8,128)(2,1)S(1)}, u32[]{:S(2)}, u32[]{:S(2)}) collective-permute-start(bf16[896,128]{1,0:T(8,128)(2,1)S(1)} %collective-permute-done.9.refs_1_), channel_id=1, source_target_pairs={{0,64},{1,65},{2,66},{3,67},{4,68},{5,69},{6,70},{7,71},{8,72},{9,... | collective-permute-start | bytes 688136 | tf_op jit(solution)/shard_map/ppermute | solution.py:39
  89.0 0.8 broadcast_select_fusion
  89.8 3.1 %collective-permute-start.3 = (bf16[896,128]{1,0:T(8,128)(2,1)}, bf16[896,128]{1,0:T(8,128)(2,1)S(1)}, u32[]{:S(2)}, u32[]{:S(2)}) collective-permute-start(bf16[896,128]{1,0:T(8,128)(2,1)} %get-tuple-element.23), channel_id=1, source_target_pairs={{0,8},{1,9},{2,10},{3,11},{4,12},{5,13},{6,14},{7,15},{8,16},{9,17... | collective-permute-start | bytes 688136 | tf_op jit(solution)/shard_map/ppermute | solution.py:39
  93.6 2.7 %collective-permute-start.4 = (bf16[896,128]{1,0:T(8,128)(2,1)}, bf16[896,128]{1,0:T(8,128)(2,1)}, u32[]{:S(2)}, u32[]{:S(2)}) collective-permute-start(bf16[896,128]{1,0:T(8,128)(2,1)} %get-tuple-element.24), channel_id=1, source_target_pairs={{0,16},{1,17},{2,18},{3,19},{4,20},{5,21},{6,22},{7,23},{8,24},{9,... | collective-permute-start | bytes 688136 | tf_op jit(solution)/shard_map/ppermute | solution.py:39
  97.0 4.6 %collective-permute-start.5 = (bf16[896,128]{1,0:T(8,128)(2,1)}, bf16[896,128]{1,0:T(8,128)(2,1)}, u32[]{:S(2)}, u32[]{:S(2)}) collective-permute-start(bf16[896,128]{1,0:T(8,128)(2,1)} %get-tuple-element.22), channel_id=1, source_target_pairs={{0,16},{1,17},{2,18},{3,19},{4,20},{5,21},{6,22},{7,23},{8,24},{9,... | collective-permute-start | bytes 688136 | tf_op jit(solution)/shard_map/ppermute | solution.py:39
  102.5 1.8 %add_convert_fusion.1.use_ref = s32[3]{0:T(128)S(1)} fusion(pred[1]{0:T(512)(128)(4,1)} %bitcast.11, pred[1]{0:T(512)(128)(4,1)} %bitcast.10, pred[1]{0:T(512)(128)(4,1)} %bitcast.9), kind=kLoop, calls=%fused_computation.8 | loop fusion | flops 9 | bytes 15 | tf_op jit(solution)/shard_map/convert_element_type | solution.py:216
  104.3 1.3 add_convert_fusion.use_ref
  105.7 3.7 %shard_map.46 = (f32[896,512]{1,0:T(8,128)S(1)}, f32[896,512]{1,0:T(8,128)S(1)}, f32[896,512]{1,0:T(8,128)S(1)}) custom-call(s32[1]{0:T(128)} %bitcast.12.place_ref, bf16[896,512]{1,0:T(8,128)(2,1)S(1)} %bitcast.40, bf16[896,128]{1,0:T(8,128)(2,1)S(1)} %bitcast.51, bf16[896,128]{1,0:T(8,128)(2,1)S(1)} %bitcast.47), custom_call_target="tpu_custom_call" | custom-call | tf_op jit(solution)/shard_map/pallas_call | solution.py:155
  109.4 0.9 copy-done.2
  110.3 0.9 copy-done.4
  111.3 7.7 %shard_map.47 = (f32[896,512]{1,0:T(8,128)S(1)}, f32[896,512]{1,0:T(8,128)S(1)}, f32[896,512]{1,0:T(8,128)S(1)}) custom-call(s32[3]{0:T(128)S(1)} %add_convert_fusion.1.use_ref, bf16[896,512]{1,0:T(8,128)(2,1)S(1)} %bitcast.41, bf16[896,128]{1,0:T(8,128)(2,1)S(1)} %collective-permute-done.8.refs_0_, bf16[896,128]{1,0:T(8,128)(2,1)S(1)} %collective-permute-done.9.refs_1_, ...), custom_call_target="tpu_custom_call" | custom-call | tf_op jit(solution)/shard_map/pallas_call | solution.py:174
  119.0 15.0 %shard_map.48 = bf16[896,512]{1,0:T(8,128)(2,1)S(1)} custom-call(s32[3]{0:T(128)S(1)} %add_convert_fusion.use_ref, bf16[896,512]{1,0:T(8,128)(2,1)S(1)} %bitcast.42, bf16[896,128]{1,0:T(8,128)(2,1)S(1)} %collective-permute-done.1.refs_0_, bf16[896,128]{1,0:T(8,128)(2,1)S(1)} %collective-permute-done.3.refs_1_, ...), custom_call_target="tpu_custom_call" | custom-call | tf_op jit(solution)/shard_map/pallas_call | solution.py:174
  134.0 30.7 %all_to_all.20 = bf16[8,112,512]{2,1,0:T(8,128)(2,1)S(1)} all-to-all(bf16[8,112,512]{2,1,0:T(8,128)(2,1)S(1)} %bitcast.43), channel_id=1, replica_groups={{0,1,2,3,4,5,6,7},{8,9,10,11,12,13,14,15},{16,17,18,19,20,21,22,23},{24..., dimensions={0} | all-to-all | bytes 1835008 | tf_op jit(solution)/shard_map/all_to_all | solution.py:27
  164.7 1.0 copy.12
  (25 shorter events, 3.0 us)
Async XLA Ops:
  0.0 0.9 copy-start
  0.0 19.0 %copy-start.5 = (bf16[112,4096]{1,0:T(8,128)(2,1)S(1)}, bf16[112,4096]{1,0:T(8,128)(2,1)}, u32[]{:S(2)}) copy-start(bf16[112,4096]{1,0:T(8,128)(2,1)} %param.4) | copy-start | bytes 2752516
  1.7 13.9 %all-to-all-start.1 = ((bf16[8,112,128]{2,1,0:T(8,128)(2,1)}), bf16[8,112,128]{2,1,0:T(8,128)(2,1)S(1)}, u32[]{:S(2)}, u32[]{:S(2)}) async-start(bf16[8,112,128]{2,1,0:T(8,128)(2,1)} %bitcast_bitcast_fusion.2), calls=%async_computation.1 | async-start | bytes 458752 | tf_op jit(solution)/shard_map/all_to_all | solution.py:27
  15.6 12.4 %all-to-all-start.2 = ((bf16[8,112,128]{2,1,0:T(8,128)(2,1)}), bf16[8,112,128]{2,1,0:T(8,128)(2,1)S(1)}, u32[]{:S(2)}, u32[]{:S(2)}) async-start(bf16[8,112,128]{2,1,0:T(8,128)(2,1)} %bitcast_bitcast_fusion.1), calls=%async_computation.2 | async-start | bytes 458752 | tf_op jit(solution)/shard_map/all_to_all | solution.py:27
  28.0 73.7 %copy-start.6 = (s32[1,3]{1,0:T(1,128)S(1)}, s32[1,3]{1,0:T(1,128)}, u32[]{:S(2)}) copy-start(s32[1,3]{1,0:T(1,128)} %param.7) | copy-start | bytes 40
  28.0 77.7 %all-to-all-start = ((bf16[8,112,512]{2,1,0:T(8,128)(2,1)}), bf16[8,112,512]{2,1,0:T(8,128)(2,1)S(1)}, u32[]{:S(2)}, u32[]{:S(2)}) async-start(bf16[8,112,512]{2,1,0:T(8,128)(2,1)} %bitcast.38), calls=%async_computation | async-start | bytes 1835008 | tf_op jit(solution)/shard_map/all_to_all | solution.py:27
  31.7 21.1 %collective-permute-start = (bf16[896,128]{1,0:T(8,128)(2,1)S(1)}, bf16[896,128]{1,0:T(8,128)(2,1)S(1)}, u32[]{:S(2)}, u32[]{:S(2)}) collective-permute-start(bf16[896,128]{1,0:T(8,128)(2,1)S(1)} %bitcast.48), channel_id=1, source_target_pairs={{0,38},{1,39},{2,36},{3,37},{4,34},{5,35},{6,32},{7,33},{8,46},{9,... | collective-permute-start | bytes 688136 | tf_op jit(solution)/shard_map/ppermute | solution.py:39
  36.4 18.5 %collective-permute-start.8 = (bf16[896,128]{1,0:T(8,128)(2,1)S(1)}, bf16[896,128]{1,0:T(8,128)(2,1)S(1)}, u32[]{:S(2)}, u32[]{:S(2)}) collective-permute-start(bf16[896,128]{1,0:T(8,128)(2,1)S(1)} %bitcast.49), channel_id=1, source_target_pairs={{0,64},{1,65},{2,66},{3,67},{4,68},{5,69},{6,70},{7,71},{8,72},{9,... | collective-permute-start | bytes 688136 | tf_op jit(solution)/shard_map/ppermute | solution.py:39
  40.7 19.0 %collective-permute-start.9 = (bf16[896,128]{1,0:T(8,128)(2,1)S(1)}, bf16[896,128]{1,0:T(8,128)(2,1)S(1)}, u32[]{:S(2)}, u32[]{:S(2)}) collective-permute-start(bf16[896,128]{1,0:T(8,128)(2,1)S(1)} %bitcast.44), channel_id=1, source_target_pairs={{0,64},{1,65},{2,66},{3,67},{4,68},{5,69},{6,70},{7,71},{8,72},{9,... | collective-permute-start | bytes 688136 | tf_op jit(solution)/shard_map/ppermute | solution.py:39
  46.2 37.2 %collective-permute-start.2 = (bf16[896,128]{1,0:T(8,128)(2,1)S(1)}, bf16[896,128]{1,0:T(8,128)(2,1)S(1)}, u32[]{:S(2)}, u32[]{:S(2)}) collective-permute-start(bf16[896,128]{1,0:T(8,128)(2,1)S(1)} %bitcast.45), channel_id=1, source_target_pairs={{0,38},{1,39},{2,36},{3,37},{4,34},{5,35},{6,32},{7,33},{8,46},{9,... | collective-permute-start | bytes 688136 | tf_op jit(solution)/shard_map/ppermute | solution.py:39
  49.5 40.3 %collective-permute-start.6 = (bf16[896,128]{1,0:T(8,128)(2,1)S(1)}, bf16[896,128]{1,0:T(8,128)(2,1)S(1)}, u32[]{:S(2)}, u32[]{:S(2)}) collective-permute-start(bf16[896,128]{1,0:T(8,128)(2,1)S(1)} %bitcast.50), channel_id=1, source_target_pairs={{0,256},{1,257},{2,258},{3,259},{4,260},{5,261},{6,262},{7,263},{8... | collective-permute-start | bytes 688136 | tf_op jit(solution)/shard_map/ppermute | solution.py:39
  52.8 66.2 %collective-permute-start.7 = (bf16[896,128]{1,0:T(8,128)(2,1)S(1)}, bf16[896,128]{1,0:T(8,128)(2,1)S(1)}, u32[]{:S(2)}, u32[]{:S(2)}) collective-permute-start(bf16[896,128]{1,0:T(8,128)(2,1)S(1)} %bitcast.46), channel_id=1, source_target_pairs={{0,256},{1,257},{2,258},{3,259},{4,260},{5,261},{6,262},{7,263},{8... | collective-permute-start | bytes 688136 | tf_op jit(solution)/shard_map/ppermute | solution.py:39
  54.9 64.1 %collective-permute-start.1 = (bf16[896,128]{1,0:T(8,128)(2,1)}, bf16[896,128]{1,0:T(8,128)(2,1)S(1)}, u32[]{:S(2)}, u32[]{:S(2)}) collective-permute-start(bf16[896,128]{1,0:T(8,128)(2,1)} %get-tuple-element.25), channel_id=1, source_target_pairs={{0,8},{1,9},{2,10},{3,11},{4,12},{5,13},{6,14},{7,15},{8,16},{9,17... | collective-permute-start | bytes 688136 | tf_op jit(solution)/shard_map/ppermute | solution.py:39
  59.7 33.2 %collective-permute-start.10 = (bf16[896,128]{1,0:T(8,128)(2,1)S(1)}, bf16[896,128]{1,0:T(8,128)(2,1)S(1)}, u32[]{:S(2)}, u32[]{:S(2)}) collective-permute-start(bf16[896,128]{1,0:T(8,128)(2,1)S(1)} %collective-permute-done.8.refs_0_), channel_id=1, source_target_pairs={{0,64},{1,65},{2,66},{3,67},{4,68},{5,69},{6,70},{7,71},{8,72},{9,... | collective-permute-start | bytes 688136 | tf_op jit(solution)/shard_map/ppermute | solution.py:39
  83.4 12.9 %collective-permute-start.11 = (bf16[896,128]{1,0:T(8,128)(2,1)S(1)}, bf16[896,128]{1,0:T(8,128)(2,1)S(1)}, u32[]{:S(2)}, u32[]{:S(2)}) collective-permute-start(bf16[896,128]{1,0:T(8,128)(2,1)S(1)} %collective-permute-done.9.refs_1_), channel_id=1, source_target_pairs={{0,64},{1,65},{2,66},{3,67},{4,68},{5,69},{6,70},{7,71},{8,72},{9,... | collective-permute-start | bytes 688136 | tf_op jit(solution)/shard_map/ppermute | solution.py:39
  89.8 29.2 %collective-permute-start.3 = (bf16[896,128]{1,0:T(8,128)(2,1)}, bf16[896,128]{1,0:T(8,128)(2,1)S(1)}, u32[]{:S(2)}, u32[]{:S(2)}) collective-permute-start(bf16[896,128]{1,0:T(8,128)(2,1)} %get-tuple-element.23), channel_id=1, source_target_pairs={{0,8},{1,9},{2,10},{3,11},{4,12},{5,13},{6,14},{7,15},{8,16},{9,17... | collective-permute-start | bytes 688136 | tf_op jit(solution)/shard_map/ppermute | solution.py:39
  92.9 0.7 copy-start.1
  93.6 25.4 %collective-permute-start.4 = (bf16[896,128]{1,0:T(8,128)(2,1)}, bf16[896,128]{1,0:T(8,128)(2,1)}, u32[]{:S(2)}, u32[]{:S(2)}) collective-permute-start(bf16[896,128]{1,0:T(8,128)(2,1)} %get-tuple-element.24), channel_id=1, source_target_pairs={{0,16},{1,17},{2,18},{3,19},{4,20},{5,21},{6,22},{7,23},{8,24},{9,... | collective-permute-start | bytes 688136 | tf_op jit(solution)/shard_map/ppermute | solution.py:39
  96.3 0.7 copy-start.3
  97.0 22.0 %collective-permute-start.5 = (bf16[896,128]{1,0:T(8,128)(2,1)}, bf16[896,128]{1,0:T(8,128)(2,1)}, u32[]{:S(2)}, u32[]{:S(2)}) collective-permute-start(bf16[896,128]{1,0:T(8,128)(2,1)} %get-tuple-element.22), channel_id=1, source_target_pairs={{0,16},{1,17},{2,18},{3,19},{4,20},{5,21},{6,22},{7,23},{8,24},{9,... | collective-permute-start | bytes 688136 | tf_op jit(solution)/shard_map/ppermute | solution.py:39
  109.4 0.9 copy-start.2
  110.3 0.9 copy-start.4

commit v2 on v1

v2 whole, which is shorter than its diff:
```python
import functools

import jax
import jax.numpy as jnp
import numpy as np
from jax import lax
from jax.experimental import pallas as pl
from jax.experimental.pallas import tpu as pltpu
from jax.sharding import PartitionSpec as P

HEAD_SIZE = 128
AXES = ("seq", "head")
SPANS, SLOTS, HALF, COLUMN = 64, 8, 4, 4
LOG_SCALE = float(HEAD_SIZE**-0.5 * np.log2(np.e))
EMPTY = -1e30
F32, BF16 = jnp.float32, jnp.bfloat16


def slot_order(span):
    if (span // COLUMN) % 2 == 0:
        return list(range(SLOTS))
    return [(SLOTS // 2 - 1 - slot // 2) * 2 + slot % 2 for slot in range(SLOTS)]


def exchange(value):
    groups = [[span * SLOTS + slot for slot in slot_order(span)] for span in range(SPANS)]
    return lax.all_to_all(
        value, AXES, split_axis=0, concat_axis=0, tiled=True, axis_index_groups=groups
    )


def moved(value, target):
    pairs = []
    for span in range(SPANS):
        goal = target(span)
        if goal is not None:
            here, there = slot_order(span), slot_order(goal)
            pairs += [(span * SLOTS + a, goal * SLOTS + b) for a, b in zip(here, there)]
    return lax.ppermute(value, AXES, pairs)


def ahead(distance):
    return lambda span: span + distance if span + distance < SPANS else None


def along_row(distance):
    return lambda span: span // COLUMN * COLUMN + (span + distance) % COLUMN


def scores_of(query, key):
    return lax.dot_general(query, key, (((1,), (1,)), ((), ())), preferred_element_type=F32)


def block_step(q_ref, key_ref, wide_ref, state):
    top_ref, total_ref, part_ref = state
    heads = q_ref.shape[1] // HEAD_SIZE
    half = q_ref.shape[0] // 2

    def rows_step(tile, _):
        rows = pl.ds(pl.multiple_of(tile * half, half), half)

        def score(head):
            return scores_of(q_ref[rows, pl.ds(head * HEAD_SIZE, HEAD_SIZE)], key_ref[...])

        following = score(0)
        for head in range(heads):
            scores = following
            if head + 1 < heads:
                following = score(head + 1)
            lanes = pl.ds(head * HEAD_SIZE, HEAD_SIZE)
            old_top = top_ref[rows, lanes]
            top = jnp.maximum(old_top, jnp.max(scores, axis=1, keepdims=True) * LOG_SCALE)
            weights = jnp.exp2(scores * LOG_SCALE - top[:, :1]).astype(BF16)
            sums = jnp.dot(weights, wide_ref[...], preferred_element_type=F32)
            factor = jnp.exp2(old_top - top)
            top_ref[rows, lanes] = top
            part_ref[rows, lanes] = part_ref[rows, lanes] * factor + sums[:, :HEAD_SIZE]
            total_ref[rows, lanes] = total_ref[rows, lanes] * factor + sums[:, HEAD_SIZE:]
        return 0

    lax.fori_loop(0, 2, rows_step, 0)


def causal_step(mirrored, q_ref, key_ref, wide_ref, state):
    top_ref, total_ref, part_ref = state
    tokens = q_ref.shape[0]
    heads = q_ref.shape[1] // HEAD_SIZE
    chunk = tokens // HALF
    order = lax.broadcasted_iota(jnp.int32, (chunk, chunk), 0)
    allowed = order >= lax.broadcasted_iota(jnp.int32, (chunk, chunk), 1)
    for turn in range(HALF):
        start = jnp.where(mirrored == 1, (HALF - 1 - turn) * chunk, turn * chunk)
        rows = pl.ds(pl.multiple_of(start, chunk), chunk)
        if turn:
            earlier = jnp.where(mirrored == 1, (HALF - turn) * chunk, 0)
            before = pl.ds(pl.multiple_of(earlier, chunk), turn * chunk)
        for head in range(heads):
            lanes = pl.ds(head * HEAD_SIZE, HEAD_SIZE)
            query = q_ref[rows, lanes]
            near = jnp.where(allowed, scores_of(query, key_ref[rows, :]), EMPTY)
            top = jnp.max(near, axis=1, keepdims=True)
            if turn:
                far = scores_of(query, key_ref[before, :])
                top = jnp.maximum(top, jnp.max(far, axis=1, keepdims=True))
            top = top * LOG_SCALE
            weights = jnp.exp2(near * LOG_SCALE - top).astype(BF16)
            sums = jnp.dot(weights, wide_ref[rows, :], preferred_element_type=F32)
            if turn:
                weights = jnp.exp2(far * LOG_SCALE - top).astype(BF16)
                sums += jnp.dot(weights, wide_ref[before, :], preferred_element_type=F32)
            top_ref[rows, lanes] = jnp.broadcast_to(top, (chunk, HEAD_SIZE))
            part_ref[rows, lanes] = sums[:, :HEAD_SIZE]
            total_ref[rows, lanes] = sums[:, HEAD_SIZE:]


def start_sources(plan_ref, sources, buffer, sem):
    tokens = buffer.shape[0] // 3
    slot = jnp.int32(0)
    for column in range(3):
        here = jnp.bool_(False)
        for kind, pieces in sources.items():
            chosen = plan_ref[column] == kind
            here = here | chosen

            @pl.when(chosen)
            def _():
                begin = 0
                for number, ref in enumerate(pieces):
                    rows = pl.ds(pl.multiple_of(slot * tokens, tokens) + begin, ref.shape[0])
                    pltpu.make_async_copy(ref, buffer.at[rows], sem).start()
                    begin += ref.shape[0]

        slot = slot + here.astype(jnp.int32)
    return slot


def earlier_blocks(found, q_ref, wide_ref, buffer, sem, state):
    tokens = buffer.shape[0] // 3
    for number in (1, 2, 3):

        @pl.when(found == number)
        def _():
            here = buffer.at[pl.ds(0, number * tokens)]
            pltpu.make_async_copy(here, here, sem).wait()

    def add(rows):
        here, wide = buffer.at[rows], wide_ref.at[pl.ds(0, rows.size)]
        wide[:, :HEAD_SIZE] = here[:, HEAD_SIZE:]
        block_step(q_ref, here.at[:, pl.ds(0, HEAD_SIZE)], wide, state)

    pl.when(found >= 2)(lambda: add(pl.ds(0, 2 * tokens)))
    odd = pl.multiple_of((found // 2) * 2 * tokens, tokens)
    pl.when(found % 2 == 1)(lambda: add(pl.ds(odd, tokens)))


def attend_kernel(plan_ref, q_ref, *refs, pieces, first, last):
    refs = list(refs)

    def take(count):
        taken, refs[:] = refs[:count], refs[count:]
        return taken

    own_ref = take(1)[0] if first else None
    sources = {kind: take(count) for kind, count in pieces}
    old = [] if first else take(2)
    if last:
        (out_ref,) = take(1)
        (new_part,) = take(1)
    else:
        rows_out, new_part = take(2)
    top_ref, total_ref, wide_ref, buffer, sem = take(5)
    state = (top_ref, total_ref, new_part)
    found = start_sources(plan_ref, sources, buffer, sem)
    wide_ref[:, HEAD_SIZE:] = jnp.ones((wide_ref.shape[0], HEAD_SIZE), BF16)
    if first:
        wide = wide_ref.at[pl.ds(0, own_ref.shape[0])]
        wide[:, :HEAD_SIZE] = own_ref[:, HEAD_SIZE:]
        causal_step(plan_ref[3], q_ref, own_ref.at[:, pl.ds(0, HEAD_SIZE)], wide, state)
    else:
        rows_buffer, part_buffer, old_sem = refs
        copies = [
            pltpu.make_async_copy(old[0], rows_buffer, old_sem.at[0]),
            pltpu.make_async_copy(old[1], part_buffer, old_sem.at[1]),
        ]
        for copy in copies:
            copy.start()
        top_ref[...] = jnp.full(top_ref.shape, EMPTY, F32)
        total_ref[...] = jnp.zeros(total_ref.shape, F32)
        new_part[...] = jnp.zeros(new_part.shape, F32)
    earlier_blocks(found, q_ref, wide_ref, buffer, sem, state)
    if not first:
        for copy in copies:
            copy.wait()
    heads = q_ref.shape[1] // HEAD_SIZE
    packed = jnp.zeros((q_ref.shape[0], HEAD_SIZE), F32)
    lane = lax.broadcasted_iota(jnp.int32, packed.shape, 1)
    for head in range(heads):
        lanes = pl.ds(head * HEAD_SIZE, HEAD_SIZE)
        top, total = top_ref[:, lanes], total_ref[:, lanes]
        if not first:
            old_top = rows_buffer[:, head : head + 1]
            old_total = rows_buffer[:, heads + head : heads + head + 1]
            both_top = jnp.maximum(old_top, top)
            before, now = jnp.exp2(old_top - both_top), jnp.exp2(top - both_top)
            top, total = both_top, old_total * before + total * now
            part = part_buffer[:, lanes] * before + new_part[:, lanes] * now
            if last:
                out_ref[:, lanes] = (part / total).astype(BF16)
            else:
                new_part[:, lanes] = part
        if not last:
            packed = jnp.where(lane == head, top, packed)
            packed = jnp.where(lane == heads + head, total, packed)
    if not last:
        rows_out[...] = packed


VMEM = pl.BlockSpec(memory_space=pltpu.VMEM)
SMEM = pl.BlockSpec(memory_space=pltpu.SMEM)
ANY = pl.BlockSpec(memory_space=pl.ANY)
PARAMS = dict(vmem_limit_bytes=40 * 2**20)


def attend(plan, query, blocks, own=None, state=None, last=False):
    tokens = query.shape[0]
    first = own is not None
    running, packed = (query.shape, F32), ((tokens, HEAD_SIZE), F32)
    result = [(query.shape, BF16)] if last else [packed, running]
    pieces = [piece for kind in blocks for piece in blocks[kind]]
    scratch = [pltpu.VMEM(*running)] * (3 if last else 2) + [
        pltpu.VMEM((2 * tokens, 2 * HEAD_SIZE), BF16),
        pltpu.VMEM((3 * tokens, 2 * HEAD_SIZE), BF16),
        pltpu.SemaphoreType.DMA,
    ]
    if not first:
        scratch += [pltpu.VMEM(*packed), pltpu.VMEM(*running), pltpu.SemaphoreType.DMA((2,))]
    counts = tuple((kind, len(blocks[kind])) for kind in blocks)
    found = pl.pallas_call(
        functools.partial(attend_kernel, pieces=counts, first=first, last=last),
        out_shape=[jax.ShapeDtypeStruct(*kind) for kind in result],
        in_specs=[SMEM, VMEM] + [VMEM] * first + [ANY] * (len(pieces) + 2 * (not first)),
        out_specs=[VMEM] * len(result),
        scratch_shapes=scratch,
        compiler_params=pltpu.CompilerParams(**PARAMS),
    )(plan, query, *([own] if first else []), *pieces, *([] if first else state))
    return found[0] if last else found


CALLS = ((4, 8, 1), (2, 16, 32))


def per_device(query_input, encoded_keys, input_values, sources):
    tokens = query_input.shape[0]
    span = lax.axis_index("seq")
    column = span % COLUMN
    mirrored = (span // COLUMN) % 2

    plan = jnp.where(sources[0] >= 0, span - sources[0], 0).astype(jnp.int32)
    plan = jnp.concatenate([plan, mirrored[None].astype(jnp.int32)])

    def slots(value):
        return value.reshape(tokens, SLOTS, -1)

    both = jnp.concatenate([slots(encoded_keys), slots(input_values)], 2).transpose(1, 0, 2)
    own = exchange(both).reshape(-1, 2 * HEAD_SIZE)
    query_cut = slots(query_input).transpose(1, 0, 2)
    four = moved(own, ahead(4))
    eight = moved(own, ahead(8))
    query = exchange(query_cut).reshape(tokens * SLOTS, -1)
    late, eight = lax.optimization_barrier((own, eight))
    blocks = {
        1: moved(jnp.where(column >= 3, four, own), along_row(1)),
        2: moved(jnp.where(column >= 2, four, own), along_row(2)),
        4: four,
        8: eight,
        16: moved(eight, ahead(8)),
        32: moved(late, ahead(32)),
    }
    blocks = {kind: [blocks[kind]] for kind in blocks}
    state = None
    for number, kinds in enumerate(CALLS):
        state = attend(
            plan,
            query,
            {kind: blocks[kind] for kind in kinds},
            own=own if number == 0 else None,
            state=state,
            last=number == len(CALLS) - 1,
        )
    back = exchange(state.reshape(SLOTS, tokens, -1))
    return back.transpose(1, 0, 2).reshape(tokens, -1)


def solution(mesh):
    in_specs = (P(AXES, None), P(AXES, None), P(AXES, None), P("seq", None))
    return jax.shard_map(
        per_device, mesh=mesh, in_specs=in_specs, out_specs=P(AXES, None), check_vma=False
    )
```

time: 167 us -> 139 us (0.83)
  the two profiles are of different devices: /device:TPU:132 before, /device:TPU:256 now
where the time goes in v2:
time: 139 us; the launch traced here: 138 us
  waiting for transfers between devices  50 us (36%)
  blocking collectives  32 us (23%)
  starting transfers between devices  28.4 us (20%)
  Pallas kernels  21.6 us (16%)
  local copies, waits for them, and re-layouts  3.98 us (3%)
  other arithmetic  1.93 us (1%)
    ppermute x6, waiting for transfers between devices, moved(): return lax.ppermute(value, AXES, pairs)  37.1 us
    all_to_all x1, blocking collectives, exchange(): lax.all_to_all(value, AXES, split_axis=0, concat_axis=0, tiled=True, axis...  32 us
    pallas_call x2, Pallas kernels, attend(): pl.pallas_call(functools.partial(attend_kernel, pieces=counts, first=firs...  21.6 us
    ppermute x6, starting transfers between devices, moved(): return lax.ppermute(value, AXES, pairs)  19.9 us
    all_to_all x2, waiting for transfers between devices, exchange(): lax.all_to_all(value, AXES, split_axis=0, concat_axis=0, tiled=True, axis...  12.9 us
    all_to_all x2, starting transfers between devices, exchange(): lax.all_to_all(value, AXES, split_axis=0, concat_axis=0, tiled=True, axis...  8.56 us
  transfers between devices with their start and end apart: 8, of which 6 were waited for; matrix products, arithmetic and copies ran while one was open for 2% of the time, Pallas kernels for 7%

profile of v2, /device:TPU:256, one launch (start us, length us, event | category | flops | bytes accessed | tf_op | source)
XLA Modules:
  0.0 138.2 jit_solution(3255167445433480242)
XLA Ops:
  0.0 0.0 copy-start
  0.0 0.0 copy-start.1
  0.0 0.9 copy-done
  0.9 1.0 copy_bitcast_fusion
  2.0 0.8 maximum_bitcast_fusion
  2.8 4.9 %all-to-all-start.1 = ((bf16[8,112,256]{2,1,0:T(8,128)(2,1)}), bf16[8,112,256]{2,1,0:T(8,128)(2,1)S(1)}, u32[]{:S(2)}, u32[]{:S(2)}) async-start(bf16[8,112,256]{2,1,0:T(8,128)(2,1)} %maximum_bitcast_fusion), calls=%async_computation.1 | async-start | bytes 917504 | tf_op jit(solution)/shard_map/all_to_all | solution.py:27
  7.7 0.0 copy-done.1
  7.7 1.0 copy.16
  8.7 12.9 %all-to-all-done.1 = bf16[8,112,256]{2,1,0:T(8,128)(2,1)S(1)} async-done(((bf16[8,112,256]{2,1,0:T(8,128)(2,1)}), bf16[8,112,256]{2,1,0:T(8,128)(2,1)S(1)}, u32[]{:S(2)}, u32[]{:S(2)}) %all-to-all-start.1) | async-done | bytes 458784 | tf_op jit(solution)/shard_map/all_to_all | solution.py:27
  21.6 0.0 copy-start.2
  21.6 3.7 %all-to-all-start = ((bf16[8,112,512]{2,1,0:T(8,128)(2,1)}), bf16[8,112,512]{2,1,0:T(8,128)(2,1)S(1)}, u32[]{:S(2)}, u32[]{:S(2)}) async-start(bf16[8,112,512]{2,1,0:T(8,128)(2,1)} %bitcast.29), calls=%async_computation | async-start | bytes 1835008 | tf_op jit(solution)/shard_map/all_to_all | solution.py:27
  25.3 4.7 %collective-permute-start = (bf16[896,256]{1,0:T(8,128)(2,1)S(1)}, bf16[896,256]{1,0:T(8,128)(2,1)S(1)}, u32[]{:S(2)}, u32[]{:S(2)}) collective-permute-start(bf16[896,256]{1,0:T(8,128)(2,1)S(1)} %bitcast.32), channel_id=1, source_target_pairs={{0,38},{1,39},{2,36},{3,37},{4,34},{5,35},{6,32},{7,33},{8,46},{9,... | collective-permute-start | bytes 1376264 | tf_op jit(solution)/shard_map/ppermute | solution.py:39
  30.0 3.4 %collective-permute-start.2 = (bf16[896,256]{1,0:T(8,128)(2,1)S(1)}, bf16[896,256]{1,0:T(8,128)(2,1)}, u32[]{:S(2)}, u32[]{:S(2)}) collective-permute-start(bf16[896,256]{1,0:T(8,128)(2,1)S(1)} %bitcast.33), channel_id=1, source_target_pairs={{0,64},{1,65},{2,66},{3,67},{4,68},{5,69},{6,70},{7,71},{8,72},{9,... | collective-permute-start | bytes 1376264 | tf_op jit(solution)/shard_map/ppermute | solution.py:39
  33.4 12.8 %collective-permute-done.refs_1_ = bf16[896,256]{1,0:T(8,128)(2,1)S(1)} collective-permute-done((bf16[896,256]{1,0:T(8,128)(2,1)S(1)}, bf16[896,256]{1,0:T(8,128)(2,1)S(1)}, u32[]{:S(2)}, u32[]{:S(2)}) %collective-permute-start) | collective-permute-done | bytes 458784 | tf_op jit(solution)/shard_map/ppermute | solution.py:39
  46.2 1.0 broadcast_select_fusion
  47.3 3.4 %collective-permute-start.5 = (bf16[896,256]{1,0:T(8,128)(2,1)}, bf16[896,256]{1,0:T(8,128)(2,1)}, u32[]{:S(2)}, u32[]{:S(2)}) collective-permute-start(bf16[896,256]{1,0:T(8,128)(2,1)} %get-tuple-element.13), channel_id=1, source_target_pairs={{0,8},{1,9},{2,10},{3,11},{4,12},{5,13},{6,14},{7,15},{8,16},{9,17... | collective-permute-start | bytes 1376264 | tf_op jit(solution)/shard_map/ppermute | solution.py:39
  50.7 2.6 %collective-permute-done.2.refs_2_ = bf16[896,256]{1,0:T(8,128)(2,1)} collective-permute-done((bf16[896,256]{1,0:T(8,128)(2,1)S(1)}, bf16[896,256]{1,0:T(8,128)(2,1)}, u32[]{:S(2)}, u32[]{:S(2)}) %collective-permute-start.2) | collective-permute-done | bytes 458784 | tf_op jit(solution)/shard_map/ppermute | solution.py:39
  53.3 4.9 %collective-permute-start.1 = (bf16[896,256]{1,0:T(8,128)(2,1)}, bf16[896,256]{1,0:T(8,128)(2,1)S(1)}, u32[]{:S(2)}, u32[]{:S(2)}) collective-permute-start(bf16[896,256]{1,0:T(8,128)(2,1)} %get-tuple-element.14), channel_id=1, source_target_pairs={{0,16},{1,17},{2,18},{3,19},{4,20},{5,21},{6,22},{7,23},{8,24},{9,... | collective-permute-start | bytes 1376264 | tf_op jit(solution)/shard_map/ppermute | solution.py:39
  58.2 2.2 %collective-permute-start.3 = (bf16[896,256]{1,0:T(8,128)(2,1)}, bf16[896,256]{1,0:T(8,128)(2,1)S(1)}, u32[]{:S(2)}, u32[]{:S(2)}) collective-permute-start(bf16[896,256]{1,0:T(8,128)(2,1)} %collective-permute-done.2.refs_2_), channel_id=1, source_target_pairs={{0,64},{1,65},{2,66},{3,67},{4,68},{5,69},{6,70},{7,71},{8,72},{9,... | collective-permute-start | bytes 1376264 | tf_op jit(solution)/shard_map/ppermute | solution.py:39
  60.4 1.3 collective-permute-start.4
  61.7 0.0 copy-done.2
  61.7 0.1 pad_add_fusion.plan_ref
  61.8 0.0 all-to-all-done
  61.8 1.4 collective-permute-done.5.refs_3_
  63.2 9.8 %shard_map.46 = (f32[896,128]{1,0:T(8,128)S(1)}, f32[896,512]{1,0:T(8,128)S(1)}) custom-call(s32[4]{0:T(128)S(1)} %pad_add_fusion.plan_ref, bf16[896,512]{1,0:T(8,128)(2,1)S(1)} %bitcast.30, bf16[896,256]{1,0:T(8,128)(2,1)S(1)} %bitcast.35, bf16[896,256]{1,0:T(8,128)(2,1)S(1)} %collective-permute-done.refs_1_, ...), custom_call_target="tpu_custom_call" | custom-call | tf_op jit(solution)/shard_map/pallas_call | solution.py:238
  73.0 0.3 collective-permute-done.1.refs_0_
  73.3 20.0 %collective-permute-done.3.refs_1_ = bf16[896,256]{1,0:T(8,128)(2,1)S(1)} collective-permute-done((bf16[896,256]{1,0:T(8,128)(2,1)}, bf16[896,256]{1,0:T(8,128)(2,1)S(1)}, u32[]{:S(2)}, u32[]{:S(2)}) %collective-permute-start.3) | collective-permute-done | bytes 458784 | tf_op jit(solution)/shard_map/ppermute | solution.py:39
  93.3 0.0 collective-permute-done.4.refs_2_
  93.4 11.8 %shard_map.47 = bf16[896,512]{1,0:T(8,128)(2,1)S(1)} custom-call(s32[4]{0:T(128)S(1)} %pad_add_fusion.plan_ref, bf16[896,512]{1,0:T(8,128)(2,1)S(1)} %bitcast.31, bf16[896,256]{1,0:T(8,128)(2,1)S(1)} %collective-permute-done.1.refs_0_, bf16[896,256]{1,0:T(8,128)(2,1)S(1)} %collective-permute-done.3.refs_1_, ...), custom_call_target="tpu_custom_call" | custom-call | tf_op jit(solution)/shard_map/pallas_call | solution.py:238
  105.1 32.0 %all_to_all.15 = bf16[8,112,512]{2,1,0:T(8,128)(2,1)S(1)} all-to-all(bf16[8,112,512]{2,1,0:T(8,128)(2,1)S(1)} %bitcast.36), channel_id=1, replica_groups={{0,1,2,3,4,5,6,7},{8,9,10,11,12,13,14,15},{16,17,18,19,20,21,22,23},{24..., dimensions={0} | all-to-all | bytes 1835008 | tf_op jit(solution)/shard_map/all_to_all | solution.py:27
  137.1 1.0 copy.12
  (1 shorter events, 0.0 us)
Async XLA Ops:
  0.0 0.9 copy-start
  0.0 7.7 %copy-start.1 = (bf16[112,4096]{1,0:T(8,128)(2,1)S(1)}, bf16[112,4096]{1,0:T(8,128)(2,1)}, u32[]{:S(2)}) copy-start(bf16[112,4096]{1,0:T(8,128)(2,1)} %param.4) | copy-start | bytes 2752516
  2.8 18.8 %all-to-all-start.1 = ((bf16[8,112,256]{2,1,0:T(8,128)(2,1)}), bf16[8,112,256]{2,1,0:T(8,128)(2,1)S(1)}, u32[]{:S(2)}, u32[]{:S(2)}) async-start(bf16[8,112,256]{2,1,0:T(8,128)(2,1)} %maximum_bitcast_fusion), calls=%async_computation.1 | async-start | bytes 917504 | tf_op jit(solution)/shard_map/all_to_all | solution.py:27
  21.6 40.1 %copy-start.2 = (s32[1,3]{1,0:T(1,128)S(1)}, s32[1,3]{1,0:T(1,128)}, u32[]{:S(2)}) copy-start(s32[1,3]{1,0:T(1,128)} %param.7) | copy-start | bytes 40
  21.6 40.2 %all-to-all-start = ((bf16[8,112,512]{2,1,0:T(8,128)(2,1)}), bf16[8,112,512]{2,1,0:T(8,128)(2,1)S(1)}, u32[]{:S(2)}, u32[]{:S(2)}) async-start(bf16[8,112,512]{2,1,0:T(8,128)(2,1)} %bitcast.29), calls=%async_computation | async-start | bytes 1835008 | tf_op jit(solution)/shard_map/all_to_all | solution.py:27
  25.3 20.9 %collective-permute-start = (bf16[896,256]{1,0:T(8,128)(2,1)S(1)}, bf16[896,256]{1,0:T(8,128)(2,1)S(1)}, u32[]{:S(2)}, u32[]{:S(2)}) collective-permute-start(bf16[896,256]{1,0:T(8,128)(2,1)S(1)} %bitcast.32), channel_id=1, source_target_pairs={{0,38},{1,39},{2,36},{3,37},{4,34},{5,35},{6,32},{7,33},{8,46},{9,... | collective-permute-start | bytes 1376264 | tf_op jit(solution)/shard_map/ppermute | solution.py:39
  30.0 23.2 %collective-permute-start.2 = (bf16[896,256]{1,0:T(8,128)(2,1)S(1)}, bf16[896,256]{1,0:T(8,128)(2,1)}, u32[]{:S(2)}, u32[]{:S(2)}) collective-permute-start(bf16[896,256]{1,0:T(8,128)(2,1)S(1)} %bitcast.33), channel_id=1, source_target_pairs={{0,64},{1,65},{2,66},{3,67},{4,68},{5,69},{6,70},{7,71},{8,72},{9,... | collective-permute-start | bytes 1376264 | tf_op jit(solution)/shard_map/ppermute | solution.py:39
  47.3 15.9 %collective-permute-start.5 = (bf16[896,256]{1,0:T(8,128)(2,1)}, bf16[896,256]{1,0:T(8,128)(2,1)}, u32[]{:S(2)}, u32[]{:S(2)}) collective-permute-start(bf16[896,256]{1,0:T(8,128)(2,1)} %get-tuple-element.13), channel_id=1, source_target_pairs={{0,8},{1,9},{2,10},{3,11},{4,12},{5,13},{6,14},{7,15},{8,16},{9,17... | collective-permute-start | bytes 1376264 | tf_op jit(solution)/shard_map/ppermute | solution.py:39
  53.3 20.0 %collective-permute-start.1 = (bf16[896,256]{1,0:T(8,128)(2,1)}, bf16[896,256]{1,0:T(8,128)(2,1)S(1)}, u32[]{:S(2)}, u32[]{:S(2)}) collective-permute-start(bf16[896,256]{1,0:T(8,128)(2,1)} %get-tuple-element.14), channel_id=1, source_target_pairs={{0,16},{1,17},{2,18},{3,19},{4,20},{5,21},{6,22},{7,23},{8,24},{9,... | collective-permute-start | bytes 1376264 | tf_op jit(solution)/shard_map/ppermute | solution.py:39
  58.2 35.1 %collective-permute-start.3 = (bf16[896,256]{1,0:T(8,128)(2,1)}, bf16[896,256]{1,0:T(8,128)(2,1)S(1)}, u32[]{:S(2)}, u32[]{:S(2)}) collective-permute-start(bf16[896,256]{1,0:T(8,128)(2,1)} %collective-permute-done.2.refs_2_), channel_id=1, source_target_pairs={{0,64},{1,65},{2,66},{3,67},{4,68},{5,69},{6,70},{7,71},{8,72},{9,... | collective-permute-start | bytes 1376264 | tf_op jit(solution)/shard_map/ppermute | solution.py:39
  60.4 33.0 %collective-permute-start.4 = (bf16[896,256]{1,0:T(8,128)(2,1)S(1)}, bf16[896,256]{1,0:T(8,128)(2,1)S(1)}, u32[]{:S(2)}, u32[]{:S(2)}) collective-permute-start(bf16[896,256]{1,0:T(8,128)(2,1)S(1)} %bitcast.34), channel_id=1, source_target_pairs={{0,256},{1,257},{2,258},{3,259},{4,260},{5,261},{6,262},{7,263},{8... | collective-permute-start | bytes 1376264 | tf_op jit(solution)/shard_map/ppermute | solution.py:39

commit v3 on v2

--- a/solution.py
+++ b/solution.py
@@ -10,7 +10,7 @@
 
 HEAD_SIZE = 128
 AXES = ("seq", "head")
-SPANS, SLOTS, HALF, COLUMN = 64, 8, 4, 4
+SPANS, SLOTS, HALF, COLUMN, PLANE = 64, 8, 4, 4, 8
 LOG_SCALE = float(HEAD_SIZE**-0.5 * np.log2(np.e))
 EMPTY = -1e30
 F32, BF16 = jnp.float32, jnp.bfloat16
@@ -45,6 +45,16 @@
 
 def along_row(distance):
     return lambda span: span // COLUMN * COLUMN + (span + distance) % COLUMN
+
+
+def behind(*planes):
+    count = SPANS // PLANE
+
+    def target(span):
+        plane = span // PLANE
+        return (plane - 2) % count * PLANE + span % PLANE if plane in planes else None
+
+    return target
 
 
 def scores_of(query, key):
@@ -246,7 +256,22 @@
     return found[0] if last else found
 
 
-CALLS = ((4, 8, 1), (2, 16, 32))
+def pass_kernel(plan_ref, block_ref, out_ref):
+    for number in range(plan_ref.shape[0]):
+        out_ref[number] = plan_ref[number]
+
+
+def passed(plan, block):
+    return pl.pallas_call(
+        pass_kernel,
+        out_shape=jax.ShapeDtypeStruct(plan.shape, plan.dtype),
+        in_specs=[SMEM, ANY],
+        out_specs=SMEM,
+        cost_estimate=pl.CostEstimate(flops=10000000000, bytes_accessed=1000000, transcendentals=0),
+    )(plan, block)
+
+
+CALLS = ((4, 8, 1), (2, 16), (32,))
 
 
 def per_device(query_input, encoded_keys, input_values, sources):
@@ -267,16 +292,16 @@
     four = moved(own, ahead(4))
     eight = moved(own, ahead(8))
     query = exchange(query_cut).reshape(tokens * SLOTS, -1)
-    late, eight = lax.optimization_barrier((own, eight))
     blocks = {
         1: moved(jnp.where(column >= 3, four, own), along_row(1)),
         2: moved(jnp.where(column >= 2, four, own), along_row(2)),
         4: four,
         8: eight,
         16: moved(eight, ahead(8)),
-        32: moved(late, ahead(32)),
+        32: moved(moved(own, behind(0, 1, 2, 3)), behind(6, 7, 0, 1)),
     }
     blocks = {kind: [blocks[kind]] for kind in blocks}
+    plan = passed(plan, blocks[1][0])
     state = None
     for number, kinds in enumerate(CALLS):
         state = attend(

time: 139 us -> 127 us (0.914)
  the two profiles are of different devices: /device:TPU:256 before, /device:TPU:62 now
where the time goes in v3:
time: 127 us; the launch traced here: 126 us
  blocking collectives  48.8 us (38%)
  starting transfers between devices  36.4 us (29%)
  Pallas kernels  26 us (20%)
  waiting for transfers between devices  8.56 us (7%)
  local copies, waits for them, and re-layouts  4.58 us (4%)
  other arithmetic  1.66 us (1%)
    all_to_all x2, blocking collectives, exchange(): lax.all_to_all(value, AXES, split_axis=0, concat_axis=0, tiled=True, axis...  48.8 us
    ppermute x7, starting transfers between devices, moved(): return lax.ppermute(value, AXES, pairs)  32.7 us
    pallas_call x3, Pallas kernels, attend(): pl.pallas_call(functools.partial(attend_kernel, pieces=counts, first=firs...  24.8 us
    ppermute x7, waiting for transfers between devices, moved(): return lax.ppermute(value, AXES, pairs)  8.56 us
    all_to_all x1, starting transfers between devices, exchange(): lax.all_to_all(value, AXES, split_axis=0, concat_axis=0, tiled=True, axis...  3.68 us
  transfers between devices with their start and end apart: 8, of which 2 were waited for; matrix products, arithmetic and copies ran while one was open for 2% of the time, Pallas kernels for 18%

profile of v3, /device:TPU:62, one launch (start us, length us, event | category | flops | bytes accessed | tf_op | source)
XLA Modules:
  0.0 126.1 jit_solution(8142309780741342559)
XLA Ops:
  0.0 0.0 copy-start
  0.0 0.9 copy-done
  0.9 1.0 copy_bitcast_fusion
  2.0 0.1 maximum_bitcast_fusion
  2.0 17.9 %all_to_all.15 = bf16[8,112,256]{2,1,0:T(8,128)(2,1)S(1)} all-to-all(bf16[8,112,256]{2,1,0:T(8,128)(2,1)S(1)} %maximum_bitcast_fusion), channel_id=1, replica_groups={{0,1,2,3,4,5,6,7},{8,9,10,11,12,13,14,15},{16,17,18,19,20,21,22,23},{24..., dimensions={0} | all-to-all | bytes 917504 | tf_op jit(solution)/shard_map/all_to_all | solution.py:27
  20.0 4.2 %collective-permute-start = (bf16[896,256]{1,0:T(8,128)(2,1)S(1)}, bf16[896,256]{1,0:T(8,128)(2,1)S(1)}, u32[]{:S(2)}, u32[]{:S(2)}) collective-permute-start(bf16[896,256]{1,0:T(8,128)(2,1)S(1)} %bitcast.33), channel_id=1, source_target_pairs={{0,38},{1,39},{2,36},{3,37},{4,34},{5,35},{6,32},{7,33},{8,46},{9,... | collective-permute-start | bytes 1376264 | tf_op jit(solution)/shard_map/ppermute | solution.py:39
  24.1 1.0 copy.16
  25.2 3.7 %all-to-all-start.1 = ((bf16[8,112,512]{2,1,0:T(8,128)(2,1)}), bf16[8,112,512]{2,1,0:T(8,128)(2,1)S(1)}, u32[]{:S(2)}, u32[]{:S(2)}) async-start(bf16[8,112,512]{2,1,0:T(8,128)(2,1)} %bitcast.29), calls=%async_computation.1 | async-start | bytes 1835008 | tf_op jit(solution)/shard_map/all_to_all | solution.py:27
  28.9 10.1 %collective-permute-start.2 = (bf16[896,256]{1,0:T(8,128)(2,1)S(1)}, bf16[896,256]{1,0:T(8,128)(2,1)}, u32[]{:S(2)}, u32[]{:S(2)}) collective-permute-start(bf16[896,256]{1,0:T(8,128)(2,1)S(1)} %bitcast.34), channel_id=1, source_target_pairs={{0,384},{1,385},{2,386},{3,387},{4,388},{5,389},{6,390},{7,391},{8... | collective-permute-start | bytes 1376264 | tf_op jit(solution)/shard_map/ppermute | solution.py:39
  38.9 2.2 %collective-permute-start.5 = (bf16[896,256]{1,0:T(8,128)(2,1)S(1)}, bf16[896,256]{1,0:T(8,128)(2,1)}, u32[]{:S(2)}, u32[]{:S(2)}) collective-permute-start(bf16[896,256]{1,0:T(8,128)(2,1)S(1)} %bitcast.35), channel_id=1, source_target_pairs={{0,64},{1,65},{2,66},{3,67},{4,68},{5,69},{6,70},{7,71},{8,72},{9,... | collective-permute-start | bytes 1376264 | tf_op jit(solution)/shard_map/ppermute | solution.py:39
  41.1 3.8 %collective-permute-done.refs_1_ = bf16[896,256]{1,0:T(8,128)(2,1)S(1)} collective-permute-done((bf16[896,256]{1,0:T(8,128)(2,1)S(1)}, bf16[896,256]{1,0:T(8,128)(2,1)S(1)}, u32[]{:S(2)}, u32[]{:S(2)}) %collective-permute-start) | collective-permute-done | bytes 458784 | tf_op jit(solution)/shard_map/ppermute | solution.py:39
  44.9 1.0 broadcast_select_fusion
  45.9 2.4 %collective-permute-start.1 = (bf16[896,256]{1,0:T(8,128)(2,1)}, bf16[896,256]{1,0:T(8,128)(2,1)}, u32[]{:S(2)}, u32[]{:S(2)}) collective-permute-start(bf16[896,256]{1,0:T(8,128)(2,1)} %get-tuple-element.14), channel_id=1, source_target_pairs={{0,8},{1,9},{2,10},{3,11},{4,12},{5,13},{6,14},{7,15},{8,16},{9,17... | collective-permute-start | bytes 1376264 | tf_op jit(solution)/shard_map/ppermute | solution.py:39
  48.3 0.6 pad_add_fusion.plan_ref
  48.9 4.3 %collective-permute-start.4 = (bf16[896,256]{1,0:T(8,128)(2,1)}, bf16[896,256]{1,0:T(8,128)(2,1)S(1)}, u32[]{:S(2)}, u32[]{:S(2)}) collective-permute-start(bf16[896,256]{1,0:T(8,128)(2,1)} %get-tuple-element.13), channel_id=1, source_target_pairs={{0,16},{1,17},{2,18},{3,19},{4,20},{5,21},{6,22},{7,23},{8,24},{9,... | collective-permute-start | bytes 1376264 | tf_op jit(solution)/shard_map/ppermute | solution.py:39
  53.2 4.8 %collective-permute-done.2 = bf16[896,256]{1,0:T(8,128)(2,1)} collective-permute-done((bf16[896,256]{1,0:T(8,128)(2,1)S(1)}, bf16[896,256]{1,0:T(8,128)(2,1)}, u32[]{:S(2)}, u32[]{:S(2)}) %collective-permute-start.2) | collective-permute-done | bytes 458784 | tf_op jit(solution)/shard_map/ppermute | solution.py:39
  58.0 6.6 %collective-permute-start.3 = (bf16[896,256]{1,0:T(8,128)(2,1)}, bf16[896,256]{1,0:T(8,128)(2,1)S(1)}, u32[]{:S(2)}, u32[]{:S(2)}) collective-permute-start(bf16[896,256]{1,0:T(8,128)(2,1)} %collective-permute-done.2), channel_id=1, source_target_pairs={{0,384},{1,385},{2,386},{3,387},{4,388},{5,389},{6,390},{7,391},{8... | collective-permute-start | bytes 1376264 | tf_op jit(solution)/shard_map/ppermute | solution.py:39
  64.6 0.0 collective-permute-done.5.refs_2_
  64.6 3.0 %collective-permute-start.6 = (bf16[896,256]{1,0:T(8,128)(2,1)}, bf16[896,256]{1,0:T(8,128)(2,1)S(1)}, u32[]{:S(2)}, u32[]{:S(2)}) collective-permute-start(bf16[896,256]{1,0:T(8,128)(2,1)} %collective-permute-done.5.refs_2_), channel_id=1, source_target_pairs={{0,64},{1,65},{2,66},{3,67},{4,68},{5,69},{6,70},{7,71},{8,72},{9,... | collective-permute-start | bytes 1376264 | tf_op jit(solution)/shard_map/ppermute | solution.py:39
  67.6 0.0 collective-permute-done.1.block_ref.refs_3_
  67.6 1.2 shard_map.46.plan_ref
  68.8 0.0 all-to-all-done.1
  68.9 0.6 copy-done.1
  69.5 13.0 %shard_map.47 = (f32[896,128]{1,0:T(8,128)S(1)}, f32[896,512]{1,0:T(8,128)S(1)}) custom-call(s32[4]{0:T(128)S(1)} %copy-done.1, bf16[896,512]{1,0:T(8,128)(2,1)S(1)} %bitcast.30, bf16[896,256]{1,0:T(8,128)(2,1)S(1)} %bitcast.36, bf16[896,256]{1,0:T(8,128)(2,1)S(1)} %collective-permute-done.refs_1_, bf16[896,256]{1,0:T(8,128)(2,1)} %collective-permute-done.5.refs_2_, ...), custom_call_target="tpu_custom_call" | custom-call | tf_op jit(solution)/shard_map/pallas_call | solution.py:248
  82.5 0.0 collective-permute-done.6.refs_1_
  82.5 0.0 collective-permute-done.4.refs_0_
  82.5 8.6 %shard_map.48 = (f32[896,128]{1,0:T(8,128)S(1)}, f32[896,512]{1,0:T(8,128)S(1)}) custom-call(s32[4]{0:T(128)S(1)} %copy-done.1, bf16[896,512]{1,0:T(8,128)(2,1)S(1)} %bitcast.31, bf16[896,256]{1,0:T(8,128)(2,1)S(1)} %collective-permute-done.4.refs_0_, bf16[896,256]{1,0:T(8,128)(2,1)S(1)} %collective-permute-done.6.refs_1_, ...), custom_call_target="tpu_custom_call" | custom-call | tf_op jit(solution)/shard_map/pallas_call | solution.py:248
  91.2 0.0 collective-permute-done.3.refs_0_
  91.2 0.0 copy-done.2
  91.2 3.1 %shard_map.49 = bf16[896,512]{1,0:T(8,128)(2,1)S(1)} custom-call(s32[4]{0:T(128)S(1)} %copy-done.2, bf16[896,512]{1,0:T(8,128)(2,1)S(1)} %bitcast.32, bf16[896,256]{1,0:T(8,128)(2,1)S(1)} %collective-permute-done.3.refs_0_, f32[896,128]{1,0:T(8,128)S(1)} %get-tuple-element.11.refs_1_, f32[896,512]{1,0:T(8,128)S(1)} %get-tuple-element.12.refs_2_), custom_call_target="tpu_custom_call" | custom-call | tf_op jit(solution)/shard_map/pallas_call | solution.py:248
  94.3 30.8 %all_to_all.16 = bf16[8,112,512]{2,1,0:T(8,128)(2,1)S(1)} all-to-all(bf16[8,112,512]{2,1,0:T(8,128)(2,1)S(1)} %bitcast.37), channel_id=1, replica_groups={{0,1,2,3,4,5,6,7},{8,9,10,11,12,13,14,15},{16,17,18,19,20,21,22,23},{24..., dimensions={0} | all-to-all | bytes 1835008 | tf_op jit(solution)/shard_map/all_to_all | solution.py:27
  125.1 1.0 copy.12
  (7 shorter events, 0.0 us)
Async XLA Ops:
  0.0 0.9 copy-start
  0.0 24.1 %copy-start.3 = (bf16[112,4096]{1,0:T(8,128)(2,1)S(1)}, bf16[112,4096]{1,0:T(8,128)(2,1)}, u32[]{:S(2)}) copy-start(bf16[112,4096]{1,0:T(8,128)(2,1)} %param.4) | copy-start | bytes 2752516
  20.0 24.9 %collective-permute-start = (bf16[896,256]{1,0:T(8,128)(2,1)S(1)}, bf16[896,256]{1,0:T(8,128)(2,1)S(1)}, u32[]{:S(2)}, u32[]{:S(2)}) collective-permute-start(bf16[896,256]{1,0:T(8,128)(2,1)S(1)} %bitcast.33), channel_id=1, source_target_pairs={{0,38},{1,39},{2,36},{3,37},{4,34},{5,35},{6,32},{7,33},{8,46},{9,... | collective-permute-start | bytes 1376264 | tf_op jit(solution)/shard_map/ppermute | solution.py:39
  25.2 23.2 %copy-start.4 = (s32[1,3]{1,0:T(1,128)S(1)}, s32[1,3]{1,0:T(1,128)}, u32[]{:S(2)}) copy-start(s32[1,3]{1,0:T(1,128)} %param.7) | copy-start | bytes 40
  25.2 43.7 %all-to-all-start.1 = ((bf16[8,112,512]{2,1,0:T(8,128)(2,1)}), bf16[8,112,512]{2,1,0:T(8,128)(2,1)S(1)}, u32[]{:S(2)}, u32[]{:S(2)}) async-start(bf16[8,112,512]{2,1,0:T(8,128)(2,1)} %bitcast.29), calls=%async_computation.1 | async-start | bytes 1835008 | tf_op jit(solution)/shard_map/all_to_all | solution.py:27
  28.9 29.1 %collective-permute-start.2 = (bf16[896,256]{1,0:T(8,128)(2,1)S(1)}, bf16[896,256]{1,0:T(8,128)(2,1)}, u32[]{:S(2)}, u32[]{:S(2)}) collective-permute-start(bf16[896,256]{1,0:T(8,128)(2,1)S(1)} %bitcast.34), channel_id=1, source_target_pairs={{0,384},{1,385},{2,386},{3,387},{4,388},{5,389},{6,390},{7,391},{8... | collective-permute-start | bytes 1376264 | tf_op jit(solution)/shard_map/ppermute | solution.py:39
  38.9 25.7 %collective-permute-start.5 = (bf16[896,256]{1,0:T(8,128)(2,1)S(1)}, bf16[896,256]{1,0:T(8,128)(2,1)}, u32[]{:S(2)}, u32[]{:S(2)}) collective-permute-start(bf16[896,256]{1,0:T(8,128)(2,1)S(1)} %bitcast.35), channel_id=1, source_target_pairs={{0,64},{1,65},{2,66},{3,67},{4,68},{5,69},{6,70},{7,71},{8,72},{9,... | collective-permute-start | bytes 1376264 | tf_op jit(solution)/shard_map/ppermute | solution.py:39
  45.9 21.7 %collective-permute-start.1 = (bf16[896,256]{1,0:T(8,128)(2,1)}, bf16[896,256]{1,0:T(8,128)(2,1)}, u32[]{:S(2)}, u32[]{:S(2)}) collective-permute-start(bf16[896,256]{1,0:T(8,128)(2,1)} %get-tuple-element.14), channel_id=1, source_target_pairs={{0,8},{1,9},{2,10},{3,11},{4,12},{5,13},{6,14},{7,15},{8,16},{9,17... | collective-permute-start | bytes 1376264 | tf_op jit(solution)/shard_map/ppermute | solution.py:39
  48.9 33.6 %collective-permute-start.4 = (bf16[896,256]{1,0:T(8,128)(2,1)}, bf16[896,256]{1,0:T(8,128)(2,1)S(1)}, u32[]{:S(2)}, u32[]{:S(2)}) collective-permute-start(bf16[896,256]{1,0:T(8,128)(2,1)} %get-tuple-element.13), channel_id=1, source_target_pairs={{0,16},{1,17},{2,18},{3,19},{4,20},{5,21},{6,22},{7,23},{8,24},{9,... | collective-permute-start | bytes 1376264 | tf_op jit(solution)/shard_map/ppermute | solution.py:39
  58.0 33.2 %collective-permute-start.3 = (bf16[896,256]{1,0:T(8,128)(2,1)}, bf16[896,256]{1,0:T(8,128)(2,1)S(1)}, u32[]{:S(2)}, u32[]{:S(2)}) collective-permute-start(bf16[896,256]{1,0:T(8,128)(2,1)} %collective-permute-done.2), channel_id=1, source_target_pairs={{0,384},{1,385},{2,386},{3,387},{4,388},{5,389},{6,390},{7,391},{8... | collective-permute-start | bytes 1376264 | tf_op jit(solution)/shard_map/ppermute | solution.py:39
  64.6 17.9 %collective-permute-start.6 = (bf16[896,256]{1,0:T(8,128)(2,1)}, bf16[896,256]{1,0:T(8,128)(2,1)S(1)}, u32[]{:S(2)}, u32[]{:S(2)}) collective-permute-start(bf16[896,256]{1,0:T(8,128)(2,1)} %collective-permute-done.5.refs_2_), channel_id=1, source_target_pairs={{0,64},{1,65},{2,66},{3,67},{4,68},{5,69},{6,70},{7,71},{8,72},{9,... | collective-permute-start | bytes 1376264 | tf_op jit(solution)/shard_map/ppermute | solution.py:39
  68.8 0.6 copy-start.1
  82.5 8.7 %copy-start.2 = (s32[4]{0:T(128)S(1)}, s32[4]{0:T(128)}, u32[]{:S(2)}) copy-start(s32[4]{0:T(128)} %shard_map.46.plan_ref) | copy-start | bytes 52

commit v4 on v3

--- a/solution.py
+++ b/solution.py
@@ -271,7 +271,7 @@
     )(plan, block)
 
 
-CALLS = ((4, 8, 1), (2, 16), (32,))
+CALLS = ((4, 8, 1), (2, 16, 32))
 
 
 def per_device(query_input, encoded_keys, input_values, sources):

time: 127 us -> 126 us (level)
  the two profiles are of different devices: /device:TPU:62 before, /device:TPU:256 now
where the time goes in v4:
time: 126 us; the launch traced here: 124 us
  blocking collectives  46 us (37%)
  starting transfers between devices  24.7 us (20%)
  waiting for transfers between devices  24 us (19%)
  Pallas kernels  22.8 us (18%)
  local copies, waits for them, and re-layouts  4.66 us (4%)
  other arithmetic  1.68 us (1%)
    all_to_all x2, blocking collectives, exchange(): lax.all_to_all(value, AXES, split_axis=0, concat_axis=0, tiled=True, axis...  46 us
    ppermute x7, waiting for transfers between devices, moved(): return lax.ppermute(value, AXES, pairs)  24 us
    pallas_call x2, Pallas kernels, attend(): pl.pallas_call(functools.partial(attend_kernel, pieces=counts, first=firs...  21.6 us
    ppermute x7, starting transfers between devices, moved(): return lax.ppermute(value, AXES, pairs)  21 us
    all_to_all x1, starting transfers between devices, exchange(): lax.all_to_all(value, AXES, split_axis=0, concat_axis=0, tiled=True, axis...  3.68 us
  transfers between devices with their start and end apart: 8, of which 3 were waited for; matrix products, arithmetic and copies ran while one was open for 2% of the time, Pallas kernels for 9%

profile of v4, /device:TPU:256, one launch (start us, length us, event | category | flops | bytes accessed | tf_op | source)
XLA Modules:
  0.0 124.0 jit_solution(12258492834978058488)
XLA Ops:
  0.0 0.0 copy-start
  0.0 0.9 copy-done
  0.9 1.0 copy_bitcast_fusion
  2.0 0.1 maximum_bitcast_fusion
  2.0 18.6 %all_to_all.15 = bf16[8,112,256]{2,1,0:T(8,128)(2,1)S(1)} all-to-all(bf16[8,112,256]{2,1,0:T(8,128)(2,1)S(1)} %maximum_bitcast_fusion), channel_id=1, replica_groups={{0,1,2,3,4,5,6,7},{8,9,10,11,12,13,14,15},{16,17,18,19,20,21,22,23},{24..., dimensions={0} | all-to-all | bytes 917504 | tf_op jit(solution)/shard_map/all_to_all | solution.py:27
  20.7 4.7 %collective-permute-start = (bf16[896,256]{1,0:T(8,128)(2,1)S(1)}, bf16[896,256]{1,0:T(8,128)(2,1)S(1)}, u32[]{:S(2)}, u32[]{:S(2)}) collective-permute-start(bf16[896,256]{1,0:T(8,128)(2,1)S(1)} %bitcast.32), channel_id=1, source_target_pairs={{0,38},{1,39},{2,36},{3,37},{4,34},{5,35},{6,32},{7,33},{8,46},{9,... | collective-permute-start | bytes 1376264 | tf_op jit(solution)/shard_map/ppermute | solution.py:39
  25.3 0.0 copy-done.3
  25.4 1.0 copy.16
  26.4 3.7 %all-to-all-start.1 = ((bf16[8,112,512]{2,1,0:T(8,128)(2,1)}), bf16[8,112,512]{2,1,0:T(8,128)(2,1)S(1)}, u32[]{:S(2)}, u32[]{:S(2)}) async-start(bf16[8,112,512]{2,1,0:T(8,128)(2,1)} %bitcast.29), calls=%async_computation.1 | async-start | bytes 1835008 | tf_op jit(solution)/shard_map/all_to_all | solution.py:27
  30.1 3.4 %collective-permute-start.3 = (bf16[896,256]{1,0:T(8,128)(2,1)S(1)}, bf16[896,256]{1,0:T(8,128)(2,1)}, u32[]{:S(2)}, u32[]{:S(2)}) collective-permute-start(bf16[896,256]{1,0:T(8,128)(2,1)S(1)} %bitcast.33), channel_id=1, source_target_pairs={{0,64},{1,65},{2,66},{3,67},{4,68},{5,69},{6,70},{7,71},{8,72},{9,... | collective-permute-start | bytes 1376264 | tf_op jit(solution)/shard_map/ppermute | solution.py:39
  33.5 1.4 %collective-permute-start.5 = (bf16[896,256]{1,0:T(8,128)(2,1)S(1)}, bf16[896,256]{1,0:T(8,128)(2,1)}, u32[]{:S(2)}, u32[]{:S(2)}) collective-permute-start(bf16[896,256]{1,0:T(8,128)(2,1)S(1)} %bitcast.34), channel_id=1, source_target_pairs={{0,384},{1,385},{2,386},{3,387},{4,388},{5,389},{6,390},{7,391},{8... | collective-permute-start | bytes 1376264 | tf_op jit(solution)/shard_map/ppermute | solution.py:39
  34.9 12.8 %collective-permute-done.refs_1_ = bf16[896,256]{1,0:T(8,128)(2,1)S(1)} collective-permute-done((bf16[896,256]{1,0:T(8,128)(2,1)S(1)}, bf16[896,256]{1,0:T(8,128)(2,1)S(1)}, u32[]{:S(2)}, u32[]{:S(2)}) %collective-permute-start) | collective-permute-done | bytes 458784 | tf_op jit(solution)/shard_map/ppermute | solution.py:39
  47.7 1.0 broadcast_select_fusion
  48.8 3.4 %collective-permute-start.1 = (bf16[896,256]{1,0:T(8,128)(2,1)}, bf16[896,256]{1,0:T(8,128)(2,1)}, u32[]{:S(2)}, u32[]{:S(2)}) collective-permute-start(bf16[896,256]{1,0:T(8,128)(2,1)} %get-tuple-element.10), channel_id=1, source_target_pairs={{0,8},{1,9},{2,10},{3,11},{4,12},{5,13},{6,14},{7,15},{8,16},{9,17... | collective-permute-start | bytes 1376264 | tf_op jit(solution)/shard_map/ppermute | solution.py:39
  52.2 0.6 pad_add_fusion.plan_ref
  52.8 4.6 %collective-permute-start.2 = (bf16[896,256]{1,0:T(8,128)(2,1)}, bf16[896,256]{1,0:T(8,128)(2,1)S(1)}, u32[]{:S(2)}, u32[]{:S(2)}) collective-permute-start(bf16[896,256]{1,0:T(8,128)(2,1)} %get-tuple-element.9), channel_id=1, source_target_pairs={{0,16},{1,17},{2,18},{3,19},{4,20},{5,21},{6,22},{7,23},{8,24},{9,... | collective-permute-start | bytes 1376264 | tf_op jit(solution)/shard_map/ppermute | solution.py:39
  57.4 0.0 collective-permute-done.3.refs_2_
  57.4 2.2 %collective-permute-start.4 = (bf16[896,256]{1,0:T(8,128)(2,1)}, bf16[896,256]{1,0:T(8,128)(2,1)S(1)}, u32[]{:S(2)}, u32[]{:S(2)}) collective-permute-start(bf16[896,256]{1,0:T(8,128)(2,1)} %collective-permute-done.3.refs_2_), channel_id=1, source_target_pairs={{0,64},{1,65},{2,66},{3,67},{4,68},{5,69},{6,70},{7,71},{8,72},{9,... | collective-permute-start | bytes 1376264 | tf_op jit(solution)/shard_map/ppermute | solution.py:39
  59.6 0.0 collective-permute-done.5
  59.6 1.3 %collective-permute-start.6 = (bf16[896,256]{1,0:T(8,128)(2,1)}, bf16[896,256]{1,0:T(8,128)(2,1)S(1)}, u32[]{:S(2)}, u32[]{:S(2)}) collective-permute-start(bf16[896,256]{1,0:T(8,128)(2,1)} %collective-permute-done.5), channel_id=1, source_target_pairs={{0,384},{1,385},{2,386},{3,387},{4,388},{5,389},{6,390},{7,391},{8... | collective-permute-start | bytes 1376264 | tf_op jit(solution)/shard_map/ppermute | solution.py:39
  60.9 3.7 %collective-permute-done.1.block_ref.refs_3_ = bf16[896,256]{1,0:T(8,128)(2,1)} collective-permute-done((bf16[896,256]{1,0:T(8,128)(2,1)}, bf16[896,256]{1,0:T(8,128)(2,1)}, u32[]{:S(2)}, u32[]{:S(2)}) %collective-permute-start.1) | collective-permute-done | bytes 458784 | tf_op jit(solution)/shard_map/ppermute | solution.py:39
  64.6 1.2 shard_map.46.plan_ref
  65.8 0.0 copy-start.2
  65.8 0.0 all-to-all-done.1
  65.8 0.7 copy-done.1
  66.5 10.0 %shard_map.47 = (f32[896,128]{1,0:T(8,128)S(1)}, f32[896,512]{1,0:T(8,128)S(1)}) custom-call(s32[4]{0:T(128)S(1)} %copy-done.1, bf16[896,512]{1,0:T(8,128)(2,1)S(1)} %bitcast.30, bf16[896,256]{1,0:T(8,128)(2,1)S(1)} %bitcast.35, bf16[896,256]{1,0:T(8,128)(2,1)S(1)} %collective-permute-done.refs_1_, bf16[896,256]{1,0:T(8,128)(2,1)} %collective-permute-done.3.refs_2_, ...), custom_call_target="tpu_custom_call" | custom-call | tf_op jit(solution)/shard_map/pallas_call | solution.py:248
  76.5 0.0 collective-permute-done.2.refs_0_
  76.5 0.0 collective-permute-done.4.refs_1_
  76.5 7.5 %collective-permute-done.6.refs_2_ = bf16[896,256]{1,0:T(8,128)(2,1)S(1)} collective-permute-done((bf16[896,256]{1,0:T(8,128)(2,1)}, bf16[896,256]{1,0:T(8,128)(2,1)S(1)}, u32[]{:S(2)}, u32[]{:S(2)}) %collective-permute-start.6) | collective-permute-done | bytes 458784 | tf_op jit(solution)/shard_map/ppermute | solution.py:39
  84.1 11.6 %shard_map.48 = bf16[896,512]{1,0:T(8,128)(2,1)S(1)} custom-call(s32[4]{0:T(128)S(1)} %copy-done.2, bf16[896,512]{1,0:T(8,128)(2,1)S(1)} %bitcast.31, bf16[896,256]{1,0:T(8,128)(2,1)S(1)} %collective-permute-done.2.refs_0_, bf16[896,256]{1,0:T(8,128)(2,1)S(1)} %collective-permute-done.4.refs_1_, bf16[896,256]{1,0:T(8,128)(2,1)S(1)} %collective-permute-done.6.refs_2_, ...), custom_call_target="tpu_custom_call" | custom-call | tf_op jit(solution)/shard_map/pallas_call | solution.py:248
  95.7 27.3 %all_to_all.16 = bf16[8,112,512]{2,1,0:T(8,128)(2,1)S(1)} all-to-all(bf16[8,112,512]{2,1,0:T(8,128)(2,1)S(1)} %bitcast.36), channel_id=1, replica_groups={{0,1,2,3,4,5,6,7},{8,9,10,11,12,13,14,15},{16,17,18,19,20,21,22,23},{24..., dimensions={0} | all-to-all | bytes 1835008 | tf_op jit(solution)/shard_map/all_to_all | solution.py:27
  123.0 1.0 copy.12
  (6 shorter events, 0.0 us)
Async XLA Ops:
  0.0 0.9 copy-start
  0.0 25.3 %copy-start.3 = (bf16[112,4096]{1,0:T(8,128)(2,1)S(1)}, bf16[112,4096]{1,0:T(8,128)(2,1)}, u32[]{:S(2)}) copy-start(bf16[112,4096]{1,0:T(8,128)(2,1)} %param.4) | copy-start | bytes 2752516
  20.7 27.1 %collective-permute-start = (bf16[896,256]{1,0:T(8,128)(2,1)S(1)}, bf16[896,256]{1,0:T(8,128)(2,1)S(1)}, u32[]{:S(2)}, u32[]{:S(2)}) collective-permute-start(bf16[896,256]{1,0:T(8,128)(2,1)S(1)} %bitcast.32), channel_id=1, source_target_pairs={{0,38},{1,39},{2,36},{3,37},{4,34},{5,35},{6,32},{7,33},{8,46},{9,... | collective-permute-start | bytes 1376264 | tf_op jit(solution)/shard_map/ppermute | solution.py:39
  26.4 25.8 %copy-start.4 = (s32[1,3]{1,0:T(1,128)S(1)}, s32[1,3]{1,0:T(1,128)}, u32[]{:S(2)}) copy-start(s32[1,3]{1,0:T(1,128)} %param.7) | copy-start | bytes 40
  26.4 39.5 %all-to-all-start.1 = ((bf16[8,112,512]{2,1,0:T(8,128)(2,1)}), bf16[8,112,512]{2,1,0:T(8,128)(2,1)S(1)}, u32[]{:S(2)}, u32[]{:S(2)}) async-start(bf16[8,112,512]{2,1,0:T(8,128)(2,1)} %bitcast.29), calls=%async_computation.1 | async-start | bytes 1835008 | tf_op jit(solution)/shard_map/all_to_all | solution.py:27
  30.1 27.4 %collective-permute-start.3 = (bf16[896,256]{1,0:T(8,128)(2,1)S(1)}, bf16[896,256]{1,0:T(8,128)(2,1)}, u32[]{:S(2)}, u32[]{:S(2)}) collective-permute-start(bf16[896,256]{1,0:T(8,128)(2,1)S(1)} %bitcast.33), channel_id=1, source_target_pairs={{0,64},{1,65},{2,66},{3,67},{4,68},{5,69},{6,70},{7,71},{8,72},{9,... | collective-permute-start | bytes 1376264 | tf_op jit(solution)/shard_map/ppermute | solution.py:39
  33.5 26.1 %collective-permute-start.5 = (bf16[896,256]{1,0:T(8,128)(2,1)S(1)}, bf16[896,256]{1,0:T(8,128)(2,1)}, u32[]{:S(2)}, u32[]{:S(2)}) collective-permute-start(bf16[896,256]{1,0:T(8,128)(2,1)S(1)} %bitcast.34), channel_id=1, source_target_pairs={{0,384},{1,385},{2,386},{3,387},{4,388},{5,389},{6,390},{7,391},{8... | collective-permute-start | bytes 1376264 | tf_op jit(solution)/shard_map/ppermute | solution.py:39
  48.8 15.9 %collective-permute-start.1 = (bf16[896,256]{1,0:T(8,128)(2,1)}, bf16[896,256]{1,0:T(8,128)(2,1)}, u32[]{:S(2)}, u32[]{:S(2)}) collective-permute-start(bf16[896,256]{1,0:T(8,128)(2,1)} %get-tuple-element.10), channel_id=1, source_target_pairs={{0,8},{1,9},{2,10},{3,11},{4,12},{5,13},{6,14},{7,15},{8,16},{9,17... | collective-permute-start | bytes 1376264 | tf_op jit(solution)/shard_map/ppermute | solution.py:39
  52.8 23.7 %collective-permute-start.2 = (bf16[896,256]{1,0:T(8,128)(2,1)}, bf16[896,256]{1,0:T(8,128)(2,1)S(1)}, u32[]{:S(2)}, u32[]{:S(2)}) collective-permute-start(bf16[896,256]{1,0:T(8,128)(2,1)} %get-tuple-element.9), channel_id=1, source_target_pairs={{0,16},{1,17},{2,18},{3,19},{4,20},{5,21},{6,22},{7,23},{8,24},{9,... | collective-permute-start | bytes 1376264 | tf_op jit(solution)/shard_map/ppermute | solution.py:39
  57.4 19.1 %collective-permute-start.4 = (bf16[896,256]{1,0:T(8,128)(2,1)}, bf16[896,256]{1,0:T(8,128)(2,1)S(1)}, u32[]{:S(2)}, u32[]{:S(2)}) collective-permute-start(bf16[896,256]{1,0:T(8,128)(2,1)} %collective-permute-done.3.refs_2_), channel_id=1, source_target_pairs={{0,64},{1,65},{2,66},{3,67},{4,68},{5,69},{6,70},{7,71},{8,72},{9,... | collective-permute-start | bytes 1376264 | tf_op jit(solution)/shard_map/ppermute | solution.py:39
  59.6 24.4 %collective-permute-start.6 = (bf16[896,256]{1,0:T(8,128)(2,1)}, bf16[896,256]{1,0:T(8,128)(2,1)S(1)}, u32[]{:S(2)}, u32[]{:S(2)}) collective-permute-start(bf16[896,256]{1,0:T(8,128)(2,1)} %collective-permute-done.5), channel_id=1, source_target_pairs={{0,384},{1,385},{2,386},{3,387},{4,388},{5,389},{6,390},{7,391},{8... | collective-permute-start | bytes 1376264 | tf_op jit(solution)/shard_map/ppermute | solution.py:39
  65.8 18.2 %copy-start.2 = (s32[4]{0:T(128)S(1)}, s32[4]{0:T(128)}, u32[]{:S(2)}) copy-start(s32[4]{0:T(128)} %shard_map.46.plan_ref) | copy-start | bytes 52
  65.8 0.7 copy-start.1
